TPU v7x, 128 devices: a whole 4x4x4 slice. The times are simulated.
128 devices in a mesh: row: 16 (over z, x_lo, core), chan: 8 (over x_hi, y).
Axes of the slice: x: 4 (x_hi: 2, x_lo: 2; x = x_hi * 2 + x_lo), y: 4, z: 4, core: 2. Of those that a mesh axis runs over, the one named last changes fastest.
Arguments:
- pair: bfloat16 [2048, 2048, 128], P('row', 'chan'), may hold values from -6 to 6
- token_mask: int32 [2048], replicated, may hold values 0 or 1
- w_left: bfloat16 [128, 256], replicated, may hold values from -0.5 to 0.5
- w_right: bfloat16 [128, 256], replicated, may hold values from -0.5 to 0.5
- w_gate: bfloat16 [128, 128], replicated, may hold values from -0.5 to 0.5
- w_out: bfloat16 [128, 128], replicated, may hold values from -0.5 to 0.5
- out_gain: float32 [128], replicated, may hold values from 0.1 to 1.9
Outputs:
- update: bfloat16 [2048, 512, 128], P('row', 'chan')
All inputs are finite; a program needn't handle non-finite values.
Results may differ from a plain program's by a relative error of at most 0.019.
Values may be sent and summed in bfloat16 or wider, within the bound.
No kernel may reach another device: no remote copies, remote signals or barrier semaphores. Data moves between devices by JAX's collectives and lax.ppermute only.
A program may use at most 256 MiB of HBM per device.

v0:
```python
import jax
import jax.numpy as jnp
from jax import lax
from jax.sharding import PartitionSpec as P

WIN_BLK = 32


def layer_norm(values):
    mean = jnp.mean(values, axis=-1, keepdims=True)
    centred = values - mean
    var = jnp.mean(centred * centred, axis=-1, keepdims=True)
    return centred * lax.rsqrt(var + 1e-05)


def project(normed, row_mask, col_mask, weight):
    rows, cols, chans = normed.shape
    both = jnp.dot(normed.reshape(rows * cols, chans), weight, preferred_element_type=jnp.float32)
    both = both.reshape(rows, cols, 2 * chans)
    gated = jax.nn.sigmoid(both[:, :, :chans]) * both[:, :, chans:]
    gated = gated * row_mask[:, None, None] * col_mask[None, :, None]
    return gated.astype(jnp.bfloat16)


def per_device(pair, token_mask, w_left, w_right, w_gate, w_out, out_gain):
    tok_rows, columns, chans = pair.shape
    maskf = token_mask.astype(jnp.float32)
    row_start = lax.axis_index("row") * tok_rows
    col_start = lax.axis_index("chan") * columns
    row_mask = lax.dynamic_slice_in_dim(maskf, row_start, tok_rows, 0)
    col_mask = lax.dynamic_slice_in_dim(maskf, col_start, columns, 0)
    normed = layer_norm(pair.astype(jnp.float32)).astype(jnp.bfloat16)
    left = project(normed, row_mask, col_mask, w_left)
    right = project(normed[:WIN_BLK], row_mask[:WIN_BLK], col_mask, w_right)
    gate_in = normed.reshape(tok_rows, columns // tok_rows, tok_rows, chans)[:, :, :WIN_BLK]
    gate_in = gate_in.reshape(-1, chans)
    gate = jnp.dot(gate_in, w_gate, preferred_element_type=jnp.float32)
    left_full, right_full = (
        lax.all_to_all(left, "chan", split_axis=2, concat_axis=1, tiled=True),
        lax.all_to_all(right, "chan", split_axis=2, concat_axis=1, tiled=True),
    )
    product = jnp.einsum(
        "ikc,jkc->ijc",
        left_full,
        lax.all_gather(right_full, "row", axis=0, tiled=True),
        preferred_element_type=jnp.float32,
    ).astype(jnp.bfloat16)
    product = lax.all_to_all(product, "chan", split_axis=1, concat_axis=2, tiled=True)
    window_cols = product.shape[1]
    normed_product = (layer_norm(product.astype(jnp.float32)) * out_gain).astype(jnp.bfloat16)
    outcome = jnp.dot(normed_product.reshape(-1, chans), w_out, preferred_element_type=jnp.float32)
    result = (jax.nn.sigmoid(gate) * outcome).astype(jnp.bfloat16)
    return result.reshape(tok_rows, window_cols, chans)


def solution(mesh):
    in_specs = (P("row", "chan", None), P(), P(), P(), P(), P(), P())
    out_specs = P("row", "chan", None)
    return jax.shard_map(
        per_device, mesh=mesh, in_specs=in_specs, out_specs=out_specs, check_vma=False
    )
```

profile of v0, /device:TPU:0, one launch (start us, length us, event | category | flops | bytes accessed | tf_op | source)
XLA Modules:
  0.0 425.6 jit_solution(413469893435256488)
XLA Ops:
  6.5 0.0 copy-start
  6.5 0.0 all-gather.2.cloned.1.call-start
  6.5 0.7 convert_element_type.49
  7.3 0.1 dynamic_slice.6
  7.3 0.1 dynamic_slice.7
  7.4 0.0 slice-start
  7.4 5.8 %convert_reduce_fusion = f32[128,256]{1,0:T(8,128)S(1)} fusion(bf16[128,256,128]{2,1,0:T(8,128)(2,1)} %param.7), kind=kLoop, calls=%fused_computation.1 | loop fusion | flops 8355840 | bytes 8519680 | tf_op jit(solution)/shard_map/reduce_sum | solution.py:10
  13.2 0.0 slice-start.1
  13.3 10.9 %fusion.2 = f32[128,256]{1,0:T(8,128)S(1)} fusion(bf16[128,256,128]{2,1,0:T(8,128)(2,1)} %param.7, f32[128,256]{1,0:T(8,128)S(1)} %broadcast_multiply_fusion), kind=kLoop, calls=%fused_computation.4 | loop fusion | flops 16744448 | bytes 8650752 | tf_op jit(solution)/shard_map/reduce_sum | solution.py:12
  24.2 0.0 slice-done
  24.2 0.0 slice-done.1
  24.2 0.0 copy-start.4
  24.2 9.9 %fusion.3 = bf16[128,256,128]{2,1,0:T(8,128)(2,1)S(1)} fusion(bf16[128,256,128]{2,1,0:T(8,128)(2,1)S(1)} %bitcast.41, f32[128,256]{1,0:T(8,128)S(1)} %add_rsqrt_fusion, f32[128,256]{1,0:T(8,128)S(1)} %broadcast_multiply_fusion), kind=kLoop, calls=%fused_computation.5 | loop fusion | flops 16777216 | bytes 17039360 | tf_op jit(solution)/shard_map/convert_element_type | solution.py:32
  34.2 0.0 copy-start.3
  34.2 3.2 copy-done.3
  37.4 0.0 copy-done.4
  37.4 1.2 fusion.25
  38.6 2.5 fusion.16
  41.1 3.4 copy.15
  44.5 35.2 %all_to_all.45 = bf16[32,256,128]{1,0,2:T(8,128)(2,1)S(1)} all-to-all(bf16[32,256,128]{1,0,2:T(8,128)(2,1)S(1)} %copy.15), channel_id=1, replica_groups=mesh['row'=16,'chan'=8] {'chan'}, dimensions={2} | all-to-all | bytes 4194304 | tf_op jit(solution)/shard_map/all_to_all | solution.py:40
  79.7 1.6 copy.25
  81.3 0.0 all-gather.2.cloned.1.call-update
  81.3 0.0 copy-done
  81.3 19.7 %fusion.23 = f32[128,256,256]{2,1,0:T(8,128)} fusion(bf16[128,256,128]{2,1,0:T(8,128)(2,1)} %copy-done.3, bf16[128,256]{1,0:T(8,128)(2,1)S(1)} %copy-done), kind=kOutput, calls=%fused_computation.35 | convolution fusion | flops 2147483648 | bytes 42008576 | tf_op jit(solution)/shard_map/dot_general | solution.py:18
  101.0 15.7 %fusion.6 = bf16[128,256,128]{2,1,0:T(8,128)(2,1)} fusion(f32[128,256,256]{2,1,0:T(8,128)} %fusion.23, f32[256]{0:T(256)S(1)} %dynamic_slice.7, f32[128]{0:T(128)S(1)} %dynamic_slice.6), kind=kLoop, calls=%fused_computation.9 | loop fusion | flops 29360128 | bytes 41944576 | tf_op jit(solution)/shard_map/convert_element_type | solution.py:22
  116.7 12.9 %copy.18 = bf16[128,256,128]{1,0,2:T(8,128)(2,1)} copy(bf16[128,256,128]{2,1,0:T(8,128)(2,1)} %fusion.6) | data formatting | bytes 16777216 | tf_op jit(solution)/shard_map/convert_element_type | solution.py:22
  129.6 191.0 %all_to_all.46 = bf16[128,256,128]{1,0,2:T(8,128)(2,1)} all-to-all(bf16[128,256,128]{1,0,2:T(8,128)(2,1)} %copy.18), channel_id=1, replica_groups=mesh['row'=16,'chan'=8] {'chan'}, dimensions={2} | all-to-all | bytes 16777216 | tf_op jit(solution)/shard_map/all_to_all | solution.py:39
  320.6 8.0 %copy.26 = bf16[8,16,16,8,256]{4,3,0,2,1:T(8,128)(2,1)} copy(bf16[8,16,16,8,256]{4,3,2,1,0:T(8,128)(2,1)} %bitcast.42) | data formatting | bytes 16777216 | tf_op jit(solution)/shard_map/all_to_all | solution.py:39
  328.5 11.3 %all-gather.2.cloned.1.call-done = bf16[512,2048,16]{1,0,2:T(8,128)(2,1)} async-done(((bf16[32,2048,16]{1,0,2:T(8,128)(2,1)}), bf16[512,2048,16]{1,0,2:T(8,128)(2,1)}) %all-gather.2.cloned.1.call-update) | async-done | bytes 33554448 | tf_op jit(solution)/shard_map/all_gather | solution.py:45
  339.8 17.7 %convert_bitcast_fusion = bf16[128,512,16]{0,1,2:T(8,128)(2,1)S(1)} fusion(bf16[512,2048,16]{1,0,2:T(8,128)(2,1)} %all-gather.2.cloned.1.call-done, bf16[128,2048,16]{1,0,2:T(8,128)(2,1)} %bitcast.44), kind=kOutput, calls=%fused_computation.33 | convolution fusion | flops 4296015872 | bytes 44040192 | tf_op jit(solution)/shard_map/ikc,jkc->ijc/dot_general | solution.py:42
  357.5 0.0 copy-start.7
  357.5 2.7 copy.21
  360.2 6.4 %all-to-all-start.2 = ((bf16[128,512,16]{0,2,1:T(8,128)(2,1)}), bf16[128,512,16]{0,2,1:T(8,128)(2,1)S(1)}, u32[]{:S(2)}, u32[]{:S(2)}) async-start(bf16[128,512,16]{0,2,1:T(8,128)(2,1)} %copy.21), calls=%async_computation.2 | async-start | bytes 4194304 | tf_op jit(solution)/shard_map/all_to_all | solution.py:48
  366.6 2.1 slice.28
  368.7 0.0 copy-done.7
  368.7 3.2 fusion.13
  371.9 21.6 %all-to-all-done.2 = bf16[128,512,16]{0,2,1:T(8,128)(2,1)S(1)} async-done(((bf16[128,512,16]{0,2,1:T(8,128)(2,1)}), bf16[128,512,16]{0,2,1:T(8,128)(2,1)S(1)}, u32[]{:S(2)}, u32[]{:S(2)}) %all-to-all-start.2) | async-done | bytes 2097184 | tf_op jit(solution)/shard_map/all_to_all | solution.py:48
  393.4 4.3 %copy.22 = f32[128,8,64,16]{2,0,3,1:T(8,128)} copy(bf16[128,8,64,16]{0,3,2,1:T(8,128)(2,1)S(1)} %bitcast.43) | data formatting | bytes 6291456 | tf_op jit(solution)/shard_map/convert_element_type | solution.py:50
  397.8 0.0 copy-start.2
  397.8 4.2 bitcast_reduce_fusion
  402.0 1.6 copy-done.2
  403.6 1.1 multiply_reduce_fusion
  404.7 0.0 copy-start.5
  404.7 0.0 copy-start.6
  404.7 0.1 div.29
  404.8 0.1 rsqrt.21
  404.9 0.0 copy-start.1
  404.9 7.9 %reshape.69 = f32[8192,128]{0,1:T(8,128)} reshape(f32[128,64,8,16]{1,0,3,2:T(8,128)} %bitcast.38) | data formatting | bytes 8388608 | tf_op jit(solution)/shard_map/convert_element_type | solution.py:50
  412.8 0.0 copy-done.5
  412.8 0.0 copy-done.6
  412.8 5.9 %fusion.12 = bf16[8192,128]{1,0:T(8,128)(2,1)} fusion(f32[8192,128]{1,0:T(8,128)} %fusion.13, bf16[128,128]{1,0:T(8,128)(2,1)S(1)} %copy-done.5, f32[8192,128]{0,1:T(8,128)} %reshape.69, f32[128]{0:T(128)S(1)} %copy-done.6, f32[8192]{0:T(1024)S(1)} %rsqrt.21, f32[8192]{0:T(1024)S(1)} %div.29), kind=kOutput, calls=%fused_computation.18 | convolution fusion | flops 274726912 | bytes 10584576 | tf_op jit(solution)/shard_map/dot_general | solution.py:51
  418.7 0.0 copy-done.1
  (5 shorter events, 0.1 us)
Async XLA Ops:
  6.5 74.8 %copy-start = (bf16[128,256]{1,0:T(8,128)(2,1)S(1)}, bf16[128,256]{1,0:T(8,128)(2,1)}, u32[]{:S(2)}) copy-start(bf16[128,256]{1,0:T(8,128)(2,1)} %param.9) | copy-start | bytes 196612
  6.5 333.3 %all-gather.2.cloned.1.call-start = ((), (), s32[]{:S(2)}) async-start(), calls=%async_computation.3 | async-start | bytes 35651584 | tf_op jit(solution)/shard_map/all_gather | solution.py:45
  7.4 16.7 %slice-start = ((s8[8388608]{0:T(1024)(128)(4,1)}), s8[4194304]{0:T(1024)(128)(4,1)S(1)}, s32[]{:S(2)}) async-start(s8[8388608]{0:T(1024)(128)(4,1)} %bitcast.40), calls=%async_computation.4 | async-start | bytes 8388608
  13.2 10.9 %slice-start.1 = ((s8[8388608]{0:T(1024)(128)(4,1)}), s8[4194304]{0:T(1024)(128)(4,1)S(1)}, s32[]{:S(2)}) async-start(s8[8388608]{0:T(1024)(128)(4,1)} %bitcast.40), calls=%async_computation.5 | async-start | bytes 8388608
  24.2 13.2 %copy-start.4 = (bf16[128,256]{1,0:T(8,128)(2,1)S(1)}, bf16[128,256]{1,0:T(8,128)(2,1)}, u32[]{:S(2)}) copy-start(bf16[128,256]{1,0:T(8,128)(2,1)} %param.10) | copy-start | bytes 196612
  34.2 3.2 copy-start.3
  357.5 11.2 %copy-start.7 = (bf16[128,128]{1,0:T(8,128)(2,1)S(1)}, bf16[128,128]{1,0:T(8,128)(2,1)}, u32[]{:S(2)}) copy-start(bf16[128,128]{1,0:T(8,128)(2,1)} %param.11) | copy-start | bytes 98308
  360.2 33.2 %all-to-all-start.2 = ((bf16[128,512,16]{0,2,1:T(8,128)(2,1)}), bf16[128,512,16]{0,2,1:T(8,128)(2,1)S(1)}, u32[]{:S(2)}, u32[]{:S(2)}) async-start(bf16[128,512,16]{0,2,1:T(8,128)(2,1)} %copy.21), calls=%async_computation.2 | async-start | bytes 4194304 | tf_op jit(solution)/shard_map/all_to_all | solution.py:48
  397.8 5.8 %copy-start.2 = (f32[128,8,64,16]{2,0,3,1:T(8,128)S(1)}, f32[128,8,64,16]{2,0,3,1:T(8,128)}, u32[]{:S(2)}) copy-start(f32[128,8,64,16]{2,0,3,1:T(8,128)} %copy.22) | copy-start | bytes 12582916
  404.7 8.1 %copy-start.5 = (bf16[128,128]{1,0:T(8,128)(2,1)S(1)}, bf16[128,128]{1,0:T(8,128)(2,1)}, u32[]{:S(2)}) copy-start(bf16[128,128]{1,0:T(8,128)(2,1)} %param.12) | copy-start | bytes 98308
  404.7 8.1 %copy-start.6 = (f32[128]{0:T(128)S(1)}, f32[128]{0:T(128)}, u32[]{:S(2)}) copy-start(f32[128]{0:T(128)} %param.13) | copy-start | bytes 1540
  404.9 13.8 %copy-start.1 = (bf16[128,256]{1,0:T(8,128)(2,1)S(1)}, bf16[128,256]{1,0:T(8,128)(2,1)}, u32[]{:S(2)}) copy-start(bf16[128,256]{1,0:T(8,128)(2,1)} %param.9) | copy-start | bytes 196612
Sparse Core Ops, SparseCore 0:
  81.4 258.3 all-gather.1
where the time goes:
time: 427 us; the launch traced here: 426 us
  blocking collectives  226 us (53%)
  other arithmetic  50.8 us (12%)
  local copies, waits for them, and re-layouts  48 us (11%)
  matrix products  47.8 us (11%)
  waiting for transfers between devices  32.8 us (8%)
  between operations  13.6 us (3%)
  starting transfers between devices  6.4 us (1%)
    all_to_all x1, blocking collectives, per_device(): lax.all_to_all(left, 'chan', split_axis=2, concat_axis=1, tiled=True)  191 us
    all_to_all x1, blocking collectives, per_device(): lax.all_to_all(right, 'chan', split_axis=2, concat_axis=1, tiled=True)  35.2 us
    all_to_all x1, waiting for transfers between devices, per_device(): lax.all_to_all(product, 'chan', split_axis=1, concat_axis=2, tiled=True)  21.6 us
    dot_general x2, matrix products, project(): jnp.dot(normed.reshape(rows * cols, chans), weight, preferred_element_typ...  21 us
    convert_element_type x2, other arithmetic, project(): return gated.astype(jnp.bfloat16)  18.1 us
    dot_general x1, matrix products, per_device(): jnp.einsum('ikc,jkc->ijc', left_full, lax.all_gather(right_full, 'row', a...  17.7 us
    convert_element_type x2, local copies, waits for them, and re-layouts, project(): return gated.astype(jnp.bfloat16)  16.3 us
    convert_element_type x2, local copies, waits for them, and re-layouts, per_device(): product.astype(jnp.float32)  12.3 us
  transfers between devices with their start and end apart: 2, of which 2 were waited for; matrix products, arithmetic and copies ran while one was open for 14% of the time, Pallas kernels for 0%

commit v1 on v0

v1 whole, which is shorter than its diff:
```python
import functools

import jax
import jax.numpy as jnp
from jax import lax
from jax.experimental import pallas as pl
from jax.experimental.pallas import tpu as pltpu
from jax.sharding import PartitionSpec as P

WIN_BLK = 32
ROW_STEP = 16
AXES = ("row", "chan")
NT = (((1,), (1,)), ((), ()))
TN = (((0,), (0,)), ((), ()))


def normed_rows(x):
    chans = x.shape[-1]
    avg = jnp.full((chans, chans), 1.0 / chans, jnp.bfloat16)
    mean = jnp.dot(x, avg, preferred_element_type=jnp.float32)
    centred = x.astype(jnp.float32) - mean
    var = jnp.dot((centred * centred).astype(jnp.bfloat16), avg, preferred_element_type=jnp.float32)
    return (centred * lax.rsqrt(var + 1e-05)).astype(jnp.bfloat16)


def project_kernel(x_ref, w_ref, mask_ref, o_ref, swap):
    rows, cols, chans = x_ref.shape
    normed = normed_rows(x_ref[...].reshape(rows * cols, chans))
    for i in range(rows):
        both = lax.dot_general(w_ref[...], normed[i * cols:(i + 1) * cols], NT, preferred_element_type=jnp.float32)
        gated = (jnp.tanh(both[:chans]) + 1.0) * both[chans:] * mask_ref[i:i + 1, :]
        for h in range(cols // 128):
            swap[h, i * chans:(i + 1) * chans, :] = gated[:, h * 128:(h + 1) * 128]
    for c in range(chans):
        for h in range(cols // 128):
            o_ref[c, :, h * 128:(h + 1) * 128] = swap[h, pl.ds(c, rows, stride=chans), :].astype(jnp.bfloat16)


def project(pair, weight, mask, first, rows):
    cols, chans = pair.shape[1:]
    weight = (0.5 * weight.T).astype(jnp.bfloat16)
    base = first // ROW_STEP
    return pl.pallas_call(
        project_kernel,
        grid=(rows // ROW_STEP,),
        in_specs=[
            pl.BlockSpec((ROW_STEP, cols, chans), lambda s: (base + s, 0, 0)),
            pl.BlockSpec((2 * chans, chans), lambda s: (0, 0)),
            pl.BlockSpec((ROW_STEP, cols), lambda s: (base + s, 0)),
        ],
        out_specs=pl.BlockSpec((chans, ROW_STEP, cols), lambda s: (0, s, 0)),
        out_shape=jax.ShapeDtypeStruct((chans, rows, cols), jnp.bfloat16),
        scratch_shapes=[pltpu.VMEM((cols // 128, ROW_STEP * chans, 128), jnp.float32)],
        compiler_params=pltpu.CompilerParams(vmem_limit_bytes=48 << 20),
    )(pair, weight, mask)


def gate_kernel(x_ref, w_ref, o_ref):
    rows, blks, blk, _, chans = x_ref.shape[0], x_ref.shape[1], WIN_BLK, 0, x_ref.shape[-1]
    normed = normed_rows(x_ref[...].reshape(rows * blks * blk, chans))
    gate = jnp.dot(normed, w_ref[...], preferred_element_type=jnp.float32)
    o_ref[...] = (0.5 * jnp.tanh(gate) + 0.5).reshape(rows, blks * blk, chans).astype(jnp.bfloat16)


def gate_of(pair, w_gate):
    rows, cols, chans = pair.shape
    blks = cols // 128
    blocks = pair.reshape(rows, blks, 128, chans)
    return pl.pallas_call(
        gate_kernel,
        grid=(rows // 32,),
        in_specs=[
            pl.BlockSpec((32, blks, WIN_BLK, chans), lambda s: (s, 0, 0, 0)),
            pl.BlockSpec((chans, chans), lambda s: (0, 0)),
        ],
        out_specs=pl.BlockSpec((32, blks * WIN_BLK, chans), lambda s: (s, 0, 0)),
        out_shape=jax.ShapeDtypeStruct((rows, blks * WIN_BLK, chans), jnp.bfloat16),
        compiler_params=pltpu.CompilerParams(vmem_limit_bytes=48 << 20),
    )(blocks, (0.5 * w_gate).astype(jnp.bfloat16))


def product_kernel(a_ref, b_ref, o_ref, acc):
    steps, parts, rows, depth = a_ref.shape
    wins, blk = b_ref.shape[0], b_ref.shape[2]
    half = rows // 2
    for q in range(parts):
        term = lax.dot_general(
            a_ref[:, q].reshape(steps * rows, depth), b_ref[:, q].reshape(wins * blk, depth), NT,
            preferred_element_type=jnp.float32)
        if q == 0:
            acc[...] = term
        else:
            acc[...] += term
    low = lax.broadcasted_iota(jnp.int32, (half, 128), 1) < 64
    for r in range(steps):
        for m in range(wins * blk // 128):
            top = acc[r * rows:r * rows + half, m * 128:(m + 1) * 128]
            bot = acc[r * rows + half:(r + 1) * rows, m * 128:(m + 1) * 128]
            o_ref[r, 2 * m] = jnp.where(low, top, pltpu.roll(bot, 64, 1)).astype(jnp.bfloat16)
            o_ref[r, 2 * m + 1] = jnp.where(low, pltpu.roll(top, 64, 1), bot).astype(jnp.bfloat16)


def product_of(left, right, n_row, n_chan):
    rows, depth = left.shape[1:]
    blk = right.shape[1]
    left = left.reshape(n_row, n_chan, rows, depth)
    right = right.reshape(n_row, n_chan, blk, depth)
    steps = 4
    out = pl.pallas_call(
        product_kernel,
        grid=(n_row // steps,),
        in_specs=[
            pl.BlockSpec((steps, n_chan, rows, depth), lambda s: (s, 0, 0, 0)),
            pl.BlockSpec((n_row, n_chan, blk, depth), lambda s: (0, 0, 0, 0)),
        ],
        out_specs=pl.BlockSpec((steps, n_chan, rows // 2, 128), lambda s: (s, 0, 0, 0)),
        out_shape=jax.ShapeDtypeStruct((n_row, n_chan, rows // 2, 128), jnp.bfloat16),
        scratch_shapes=[pltpu.VMEM((steps * rows, n_row * blk), jnp.float32)],
        compiler_params=pltpu.CompilerParams(vmem_limit_bytes=48 << 20),
    )(left, right)
    return out.reshape(n_row * n_chan, rows // 2, 128)


def finish_kernel(p_ref, gain_ref, w_ref, gate_ref, o_ref, swap):
    chans, subs, lanes = p_ref.shape
    x = p_ref[...].astype(jnp.float32)
    mean = jnp.sum(x, axis=0) * (1.0 / chans)
    centred = x - mean[None]
    var = jnp.sum(centred * centred, axis=0) * (1.0 / chans)
    swap[...] = (centred * lax.rsqrt(var + 1e-05)[None]).reshape(chans * subs, lanes)
    half = lanes // 2
    for s in range(subs):
        normed = (swap[pl.ds(s, chans, stride=subs), :] * gain_ref[...]).astype(jnp.bfloat16)
        outcome = lax.dot_general(normed, w_ref[...], TN, preferred_element_type=jnp.float32)
        for h in range(2):
            gate = gate_ref[h, s].astype(jnp.float32)
            o_ref[h, s] = (gate * outcome[h * half:(h + 1) * half]).astype(jnp.bfloat16)


def finish(product, out_gain, w_out, gate):
    chans, subs, lanes = product.shape
    rows, wins = gate.shape[:2]
    step = 16
    out = pl.pallas_call(
        finish_kernel,
        grid=(subs // step,),
        in_specs=[
            pl.BlockSpec((chans, step, lanes), lambda s: (0, s, 0)),
            pl.BlockSpec((chans, 1), lambda s: (0, 0)),
            pl.BlockSpec((chans, chans), lambda s: (0, 0)),
            pl.BlockSpec((2, step, wins, chans), lambda s: (0, s, 0, 0)),
        ],
        out_specs=pl.BlockSpec((2, step, wins, chans), lambda s: (0, s, 0, 0)),
        out_shape=jax.ShapeDtypeStruct((2, subs, wins, chans), jnp.bfloat16),
        scratch_shapes=[pltpu.VMEM((chans * step, lanes), jnp.float32)],
        compiler_params=pltpu.CompilerParams(vmem_limit_bytes=48 << 20),
    )(product, out_gain.reshape(chans, 1), w_out, gate.reshape(2, subs, wins, chans))
    return out.reshape(rows, wins, chans)


def spread(values):
    return lax.all_to_all(values, AXES, split_axis=0, concat_axis=0, tiled=True)


def per_device(n_row, n_chan, pair, token_mask, w_left, w_right, w_gate, w_out, out_gain):
    tok_rows, columns, chans = pair.shape
    maskf = token_mask.astype(jnp.float32)
    row_mask = lax.dynamic_slice_in_dim(maskf, lax.axis_index("row") * tok_rows, tok_rows, 0)
    col_mask = lax.dynamic_slice_in_dim(maskf, lax.axis_index("chan") * columns, columns, 0)
    mask = row_mask[:, None] * col_mask[None, :]
    right = spread(project(pair, w_right, mask, 0, WIN_BLK))
    left = spread(project(pair, w_left, mask, 0, tok_rows))
    gate = gate_of(pair, w_gate)
    product = spread(product_of(left, right, n_row, n_chan))
    return finish(product, out_gain, w_out, gate)


def solution(mesh):
    in_specs = (P("row", "chan", None), P(), P(), P(), P(), P(), P())
    out_specs = P("row", "chan", None)
    body = functools.partial(per_device, mesh.shape["row"], mesh.shape["chan"])
    return jax.shard_map(
        body, mesh=mesh, in_specs=in_specs, out_specs=out_specs, check_vma=False
    )
```

time: 427 us -> 208 us (0.49)
  blocking collectives: 226 us -> 104 us
  Pallas kernels: 0 us -> 52.3 us
  other arithmetic: 50.8 us -> 0.8 us
  matrix products: 47.8 us -> 0 us
  local copies, waits for them, and re-layouts: 48 us -> 3.97 us
  between operations: 13.6 us -> 0.13 us
  starting transfers between devices: 6.4 us -> 17.6 us
    all_to_all x2 -> x1, blocking collectives: 226 us -> 104 us  [spread(): return lax.all_to_all(values, AXES, split_axis=0, concat_axis=0, tiled=True)]
    pallas_call x0 -> x5, Pallas kernels: none -> 52.3 us  [the longest x2 33.9 us: project(): pl.pallas_call(project_kernel, grid=(rows // ROW_STEP,), in_specs=[pl.Blo...]
    dot_general x5 -> x0, matrix products: 47.8 us -> none  [the longest x2 21 us: project(): jnp.dot(normed.reshape(rows * cols, chans), weight, preferred_element_typ...]
    convert_element_type x5 -> x0, local copies, waits for them, and re-layouts: 31.2 us -> none  [the longest x2 16.3 us: project(): return gated.astype(jnp.bfloat16)]
    convert_element_type x3 -> x0, other arithmetic: 28.1 us -> none  [the longest x2 18.1 us: project(): return gated.astype(jnp.bfloat16)]
    reduce_sum x4 -> x0, other arithmetic: 22 us -> none  [the longest x2 12 us: layer_norm(): var = jnp.mean(centred * centred, axis=-1, keepdims=True)]
    all_gather x1 -> x0, waiting for transfers between devices: 11.3 us -> none  [per_device(): lax.all_gather(right_full, 'row', axis=0, tiled=True)]
    all_to_all x1 -> x2, starting transfers between devices: 6.4 us -> 17.6 us  [spread(): return lax.all_to_all(values, AXES, split_axis=0, concat_axis=0, tiled=True)]
  transfers between devices with their start and end apart: 2 -> 2, of which waited for: 2 -> 2; matrix products, arithmetic and copies ran while one was open for 14% -> 0% of each run, Pallas kernels for 0% -> 15%
where the time goes in v1:
time: 208 us; the launch traced here: 207 us
  blocking collectives  104 us (50%)
  Pallas kernels  52.3 us (25%)
  waiting for transfers between devices  28.8 us (14%)
  starting transfers between devices  17.6 us (8%)
  local copies, waits for them, and re-layouts  3.97 us (2%)
    all_to_all x1, blocking collectives, spread(): return lax.all_to_all(values, AXES, split_axis=0, concat_axis=0, tiled=True)  104 us
    pallas_call x2, Pallas kernels, project(): pl.pallas_call(project_kernel, grid=(rows // ROW_STEP,), in_specs=[pl.Blo...  33.9 us
    all_to_all x2, waiting for transfers between devices, spread(): return lax.all_to_all(values, AXES, split_axis=0, concat_axis=0, tiled=True)  28.8 us
    all_to_all x2, starting transfers between devices, spread(): return lax.all_to_all(values, AXES, split_axis=0, concat_axis=0, tiled=True)  17.6 us
    pallas_call x1, Pallas kernels, product_of(): pl.pallas_call(product_kernel, grid=(n_row // steps,), in_specs=[pl.Block...  7.34 us
    pallas_call x1, Pallas kernels, finish(): pl.pallas_call(finish_kernel, grid=(subs // step,), in_specs=[pl.BlockSpe...  6.69 us
    pallas_call x1, Pallas kernels, gate_of(): pl.pallas_call(gate_kernel, grid=(rows // 32,), in_specs=[pl.BlockSpec((3...  4.29 us
  transfers between devices with their start and end apart: 2, of which 2 were waited for; matrix products, arithmetic and copies ran while one was open for 0% of the time, Pallas kernels for 15%

profile of v1, /device:TPU:0, one launch (start us, length us, event | category | flops | bytes accessed | tf_op | source)
XLA Modules:
  0.0 207.5 jit_solution(3933988216454133382)
XLA Ops:
  0.0 0.7 convert_element_type.3
  0.7 0.1 dynamic_slice.6
  0.8 0.1 dynamic_slice.7
  0.8 0.9 copy.9
  1.8 0.1 broadcast_multiply_fusion.mask_ref
  1.9 7.4 %shard_map.74 = bf16[128,32,256]{2,1,0:T(8,128)(2,1)S(1)} custom-call(bf16[128,256,128]{2,1,0:T(8,128)(2,1)} %x_ref.3, bf16[256,128]{1,0:T(8,128)(2,1)S(1)} %multiply_bitcast_fusion.w_ref, f32[128,256]{1,0:T(8,128)S(1)} %broadcast_multiply_fusion.mask_ref), custom_call_target="tpu_custom_call" | custom-call | tf_op jit(solution)/shard_map/pallas_call | solution.py:43
  9.4 0.0 copy-start
  9.4 1.3 copy-done
  10.7 0.0 copy-start.3
  10.7 11.1 %all-to-all-start.1 = ((bf16[128,32,256]{2,1,0:T(8,128)(2,1)}), bf16[128,32,256]{2,1,0:T(8,128)(2,1)S(1)}, u32[]{:S(2)}, u32[]{:S(2)}) async-start(bf16[128,32,256]{2,1,0:T(8,128)(2,1)} %copy-done), calls=%async_computation.1 | async-start | bytes 4194304 | tf_op jit(solution)/shard_map/all_to_all | solution.py:162
  21.8 0.0 copy-done.3
  21.8 0.1 copy.8
  22.0 26.5 %shard_map.73 = bf16[128,128,256]{2,1,0:T(8,128)(2,1)} custom-call(bf16[128,256,128]{2,1,0:T(8,128)(2,1)} %x_ref.3, bf16[256,128]{1,0:T(8,128)(2,1)S(1)} %multiply_bitcast_fusion.1.w_ref, f32[128,256]{1,0:T(8,128)S(1)} %broadcast_multiply_fusion.mask_ref), custom_call_target="tpu_custom_call" | custom-call | tf_op jit(solution)/shard_map/pallas_call | solution.py:43
  48.5 3.5 %all-to-all-done.1 = bf16[128,32,256]{2,1,0:T(8,128)(2,1)S(1)} async-done(((bf16[128,32,256]{2,1,0:T(8,128)(2,1)}), bf16[128,32,256]{2,1,0:T(8,128)(2,1)S(1)}, u32[]{:S(2)}, u32[]{:S(2)}) %all-to-all-start.1) | async-done | bytes 2097184 | tf_op jit(solution)/shard_map/all_to_all | solution.py:162
  52.0 103.9 %all_to_all.15 = bf16[128,128,256]{2,1,0:T(8,128)(2,1)} all-to-all(bf16[128,128,256]{2,1,0:T(8,128)(2,1)} %shard_map.73), channel_id=1, replica_groups=mesh['row'=16,'chan'=8] {'row','chan'}, dimensions={0} | all-to-all | bytes 16777216 | tf_op jit(solution)/shard_map/all_to_all | solution.py:162
  155.9 7.3 %shard_map.75 = bf16[16,8,64,128]{3,2,1,0:T(8,128)(2,1)S(1)} custom-call(bf16[16,8,128,256]{3,2,1,0:T(8,128)(2,1)} %bitcast.15, bf16[16,8,32,256]{3,2,1,0:T(8,128)(2,1)S(1)} %bitcast.12), custom_call_target="tpu_custom_call" | custom-call | tf_op jit(solution)/shard_map/pallas_call | solution.py:109
  163.2 0.0 copy-start.1
  163.3 1.3 copy-done.1
  164.6 0.0 copy-start.5
  164.6 0.0 copy-start.4
  164.6 6.4 %all-to-all-start.2 = ((bf16[128,64,128]{2,1,0:T(8,128)(2,1)}), bf16[128,64,128]{2,1,0:T(8,128)(2,1)}, u32[]{:S(2)}, u32[]{:S(2)}) async-start(bf16[128,64,128]{2,1,0:T(8,128)(2,1)} %bitcast.13), calls=%async_computation.2 | async-start | bytes 4194304 | tf_op jit(solution)/shard_map/all_to_all | solution.py:162
  171.0 0.0 copy-done.5
  171.0 0.1 copy.10.gain_ref
  171.1 0.0 copy-done.4
  171.2 0.0 copy-start.2
  171.2 4.3 %shard_map.76 = bf16[128,64,128]{2,1,0:T(8,128)(2,1)S(1)} custom-call(bf16[128,2,128,128]{3,2,1,0:T(8,128)(2,1)} %bitcast.14, bf16[128,128]{1,0:T(8,128)(2,1)S(1)} %broadcast_multiply_fusion.1.w_ref), custom_call_target="tpu_custom_call" | custom-call | tf_op jit(solution)/shard_map/pallas_call | solution.py:69
  175.5 25.3 %all-to-all-done.2.p_ref = bf16[128,64,128]{2,1,0:T(8,128)(2,1)} async-done(((bf16[128,64,128]{2,1,0:T(8,128)(2,1)}), bf16[128,64,128]{2,1,0:T(8,128)(2,1)}, u32[]{:S(2)}, u32[]{:S(2)}) %all-to-all-start.2) | async-done | bytes 2097184 | tf_op jit(solution)/shard_map/all_to_all | solution.py:162
  200.8 0.0 copy-done.2
  200.8 6.7 %shard_map.77 = bf16[2,64,64,128]{3,2,1,0:T(8,128)(2,1)} custom-call(bf16[128,64,128]{2,1,0:T(8,128)(2,1)} %all-to-all-done.2.p_ref, f32[128,1]{1,0:T(8,128)S(1)} %copy.10.gain_ref, bf16[128,128]{1,0:T(8,128)(2,1)S(1)} %copy-done.2, bf16[2,64,64,128]{3,2,1,0:T(8,128)(2,1)S(1)} %bitcast.11), custom_call_target="tpu_custom_call" | custom-call | tf_op jit(solution)/shard_map/pallas_call | solution.py:144
  (3 shorter events, 0.0 us)
Async XLA Ops:
  9.4 1.3 copy-start
  10.7 11.2 %copy-start.3 = (bf16[128,256]{1,0:T(8,128)(2,1)S(1)}, bf16[128,256]{1,0:T(8,128)(2,1)}, u32[]{:S(2)}) copy-start(bf16[128,256]{1,0:T(8,128)(2,1)} %param.9) | copy-start | bytes 196612
  10.7 41.3 %all-to-all-start.1 = ((bf16[128,32,256]{2,1,0:T(8,128)(2,1)}), bf16[128,32,256]{2,1,0:T(8,128)(2,1)S(1)}, u32[]{:S(2)}, u32[]{:S(2)}) async-start(bf16[128,32,256]{2,1,0:T(8,128)(2,1)} %copy-done), calls=%async_computation.1 | async-start | bytes 4194304 | tf_op jit(solution)/shard_map/all_to_all | solution.py:162
  163.2 1.3 copy-start.1
  164.6 6.4 %copy-start.5 = (f32[128]{0:T(128)S(1)}, f32[128]{0:T(128)}, u32[]{:S(2)}) copy-start(f32[128]{0:T(128)} %param.13) | copy-start | bytes 1540
  164.6 6.6 %copy-start.4 = (bf16[128,128]{1,0:T(8,128)(2,1)S(1)}, bf16[128,128]{1,0:T(8,128)(2,1)}, u32[]{:S(2)}) copy-start(bf16[128,128]{1,0:T(8,128)(2,1)} %param.11) | copy-start | bytes 98308
  164.6 36.2 %all-to-all-start.2 = ((bf16[128,64,128]{2,1,0:T(8,128)(2,1)}), bf16[128,64,128]{2,1,0:T(8,128)(2,1)}, u32[]{:S(2)}, u32[]{:S(2)}) async-start(bf16[128,64,128]{2,1,0:T(8,128)(2,1)} %bitcast.13), calls=%async_computation.2 | async-start | bytes 4194304 | tf_op jit(solution)/shard_map/all_to_all | solution.py:162
  171.2 29.6 %copy-start.2 = (bf16[128,128]{1,0:T(8,128)(2,1)S(1)}, bf16[128,128]{1,0:T(8,128)(2,1)}, u32[]{:S(2)}) copy-start(bf16[128,128]{1,0:T(8,128)(2,1)} %w_ref.1) | copy-start | bytes 98308

commit v2 on v1

--- a/solution.py
+++ b/solution.py
@@ -1,15 +1,16 @@
-import functools
-
 import jax
 import jax.numpy as jnp
 from jax import lax
 from jax.experimental import pallas as pl
 from jax.experimental.pallas import tpu as pltpu
-from jax.sharding import PartitionSpec as P
+from jax.sharding import Mesh, PartitionSpec as P
 
 WIN_BLK = 32
 ROW_STEP = 16
-AXES = ("row", "chan")
+N_ROW = 16
+ROW = ("z", "x_lo", "core")
+CHAN = ("x_hi", "y")
+PLANE = ("x_lo", "core", "x_hi", "y")
 NT = (((1,), (1,)), ((), ()))
 TN = (((0,), (0,)), ((), ()))
 
@@ -81,11 +82,12 @@
 
 def product_kernel(a_ref, b_ref, o_ref, acc):
     steps, parts, rows, depth = a_ref.shape
-    wins, blk = b_ref.shape[0], b_ref.shape[2]
+    planes, per_plane, _, blk, _ = b_ref.shape
+    wins = planes * per_plane * blk
     half = rows // 2
     for q in range(parts):
         term = lax.dot_general(
-            a_ref[:, q].reshape(steps * rows, depth), b_ref[:, q].reshape(wins * blk, depth), NT,
+            a_ref[:, q].reshape(steps * rows, depth), b_ref[:, :, q].reshape(wins, depth), NT,
             preferred_element_type=jnp.float32)
         if q == 0:
             acc[...] = term
@@ -93,32 +95,33 @@
             acc[...] += term
     low = lax.broadcasted_iota(jnp.int32, (half, 128), 1) < 64
     for r in range(steps):
-        for m in range(wins * blk // 128):
+        for m in range(wins // 128):
             top = acc[r * rows:r * rows + half, m * 128:(m + 1) * 128]
             bot = acc[r * rows + half:(r + 1) * rows, m * 128:(m + 1) * 128]
             o_ref[r, 2 * m] = jnp.where(low, top, pltpu.roll(bot, 64, 1)).astype(jnp.bfloat16)
             o_ref[r, 2 * m + 1] = jnp.where(low, pltpu.roll(top, 64, 1), bot).astype(jnp.bfloat16)
 
 
-def product_of(left, right, n_row, n_chan):
+def product_of(left, right, n_chan):
     rows, depth = left.shape[1:]
-    blk = right.shape[1]
-    left = left.reshape(n_row, n_chan, rows, depth)
-    right = right.reshape(n_row, n_chan, blk, depth)
-    steps = 4
+    planes, blk = right.shape[0], right.shape[2]
+    steps = N_ROW // planes
+    own = left.shape[0] // (steps * n_chan)
+    left = left.reshape(steps, n_chan, own, rows, depth)
+    right = right.reshape(planes, steps, n_chan, own, blk, depth)
     out = pl.pallas_call(
         product_kernel,
-        grid=(n_row // steps,),
+        grid=(own,),
         in_specs=[
-            pl.BlockSpec((steps, n_chan, rows, depth), lambda s: (s, 0, 0, 0)),
-            pl.BlockSpec((n_row, n_chan, blk, depth), lambda s: (0, 0, 0, 0)),
+            pl.BlockSpec((steps, n_chan, None, rows, depth), lambda c: (0, 0, c, 0, 0)),
+            pl.BlockSpec((planes, steps, n_chan, None, blk, depth), lambda c: (0, 0, 0, c, 0, 0)),
         ],
-        out_specs=pl.BlockSpec((steps, n_chan, rows // 2, 128), lambda s: (s, 0, 0, 0)),
-        out_shape=jax.ShapeDtypeStruct((n_row, n_chan, rows // 2, 128), jnp.bfloat16),
-        scratch_shapes=[pltpu.VMEM((steps * rows, n_row * blk), jnp.float32)],
+        out_specs=pl.BlockSpec((steps, n_chan, None, rows // 2, 128), lambda c: (0, 0, c, 0, 0)),
+        out_shape=jax.ShapeDtypeStruct((steps, n_chan, own, rows // 2, 128), jnp.bfloat16),
+        scratch_shapes=[pltpu.VMEM((steps * rows, N_ROW * blk), jnp.float32)],
         compiler_params=pltpu.CompilerParams(vmem_limit_bytes=48 << 20),
     )(left, right)
-    return out.reshape(n_row * n_chan, rows // 2, 128)
+    return out.reshape(-1, rows // 2, 128)
 
 
 def finish_kernel(p_ref, gain_ref, w_ref, gate_ref, o_ref, swap):
@@ -159,26 +162,29 @@
 
 
 def spread(values):
-    return lax.all_to_all(values, AXES, split_axis=0, concat_axis=0, tiled=True)
+    return lax.all_to_all(values, PLANE, split_axis=0, concat_axis=0, tiled=True)
 
 
-def per_device(n_row, n_chan, pair, token_mask, w_left, w_right, w_gate, w_out, out_gain):
+def per_device(pair, token_mask, w_left, w_right, w_gate, w_out, out_gain):
     tok_rows, columns, chans = pair.shape
     maskf = token_mask.astype(jnp.float32)
-    row_mask = lax.dynamic_slice_in_dim(maskf, lax.axis_index("row") * tok_rows, tok_rows, 0)
-    col_mask = lax.dynamic_slice_in_dim(maskf, lax.axis_index("chan") * columns, columns, 0)
+    row_mask = lax.dynamic_slice_in_dim(maskf, lax.axis_index(ROW) * tok_rows, tok_rows, 0)
+    col_mask = lax.dynamic_slice_in_dim(maskf, lax.axis_index(CHAN) * columns, columns, 0)
     mask = row_mask[:, None] * col_mask[None, :]
     right = spread(project(pair, w_right, mask, 0, WIN_BLK))
-    left = spread(project(pair, w_left, mask, 0, tok_rows))
+    left = project(pair, w_left, mask, 0, tok_rows)
+    right, left = lax.optimization_barrier((right, left))
+    right = lax.all_gather(right, "z", axis=0)
+    left = spread(left)
     gate = gate_of(pair, w_gate)
-    product = spread(product_of(left, right, n_row, n_chan))
+    product = spread(product_of(left, right, maskf.shape[0] // columns))
     return finish(product, out_gain, w_out, gate)
 
 
 def solution(mesh):
-    in_specs = (P("row", "chan", None), P(), P(), P(), P(), P(), P())
-    out_specs = P("row", "chan", None)
-    body = functools.partial(per_device, mesh.shape["row"], mesh.shape["chan"])
+    by_axis = Mesh(mesh.devices.reshape(4, 2, 2, 2, 4), ROW + CHAN)
+    in_specs = (P(ROW, CHAN, None), P(), P(), P(), P(), P(), P())
+    out_specs = P(ROW, CHAN, None)
     return jax.shard_map(
-        body, mesh=mesh, in_specs=in_specs, out_specs=out_specs, check_vma=False
+        per_device, mesh=by_axis, in_specs=in_specs, out_specs=out_specs, check_vma=False
     )

time: 208 us -> 215 us (1.034)
  between operations: 0.13 us -> 13.5 us
  starting transfers between devices: 17.6 us -> 12.5 us
  waiting for transfers between devices: 28.8 us -> 24.8 us
  Pallas kernels: 52.3 us -> 55.5 us
    all_to_all x2, starting transfers between devices: 17.6 us -> 12.4 us  [spread(): lax.all_to_all(values, PLANE, split_axis=0, concat_axis=0, tiled=True)]
    all_to_all x2, waiting for transfers between devices: 28.8 us -> 24.8 us  [spread(): lax.all_to_all(values, PLANE, split_axis=0, concat_axis=0, tiled=True)]
    pallas_call x1, Pallas kernels: 7.34 us -> 9.83 us  [product_of(): pl.pallas_call(product_kernel, grid=(own,), in_specs=[pl.BlockSpec((steps...]
  transfers between devices with their start and end apart: 2 -> 3, of which waited for: 2 -> 2; matrix products, arithmetic and copies ran while one was open for 0% -> 0% of each run, Pallas kernels for 15% -> 14%
where the time goes in v2:
time: 215 us; the launch traced here: 214 us
  blocking collectives  104 us (48%)
  Pallas kernels  55.5 us (26%)
  waiting for transfers between devices  24.8 us (12%)
  between operations  13.5 us (6%)
  starting transfers between devices  12.5 us (6%)
  local copies, waits for them, and re-layouts  2.66 us (1%)
    all_to_all x1, blocking collectives, spread(): lax.all_to_all(values, PLANE, split_axis=0, concat_axis=0, tiled=True)  104 us
    pallas_call x2, Pallas kernels, project(): pl.pallas_call(project_kernel, grid=(rows // ROW_STEP,), in_specs=[pl.Blo...  34.7 us
    all_to_all x2, waiting for transfers between devices, spread(): lax.all_to_all(values, PLANE, split_axis=0, concat_axis=0, tiled=True)  24.8 us
    all_to_all x2, starting transfers between devices, spread(): lax.all_to_all(values, PLANE, split_axis=0, concat_axis=0, tiled=True)  12.4 us
    pallas_call x1, Pallas kernels, product_of(): pl.pallas_call(product_kernel, grid=(own,), in_specs=[pl.BlockSpec((steps...  9.83 us
    pallas_call x1, Pallas kernels, finish(): pl.pallas_call(finish_kernel, grid=(subs // step,), in_specs=[pl.BlockSpe...  6.69 us
  transfers between devices with their start and end apart: 3, of which 2 were waited for; matrix products, arithmetic and copies ran while one was open for 0% of the time, Pallas kernels for 14%

profile of v2, /device:TPU:0, one launch (start us, length us, event | category | flops | bytes accessed | tf_op | source)
XLA Modules:
  0.0 214.0 jit_solution(13675589069977381481)
XLA Ops:
  6.5 0.7 convert_element_type.3
  7.2 0.1 dynamic_slice.6
  7.3 0.1 dynamic_slice.7
  7.4 0.9 copy.11
  8.4 0.1 broadcast_multiply_fusion.mask_ref
  8.4 8.2 %shard_map.73 = bf16[128,32,256]{2,1,0:T(8,128)(2,1)} custom-call(bf16[128,256,128]{2,1,0:T(8,128)(2,1)} %x_ref.3, bf16[256,128]{1,0:T(8,128)(2,1)S(1)} %multiply_bitcast_fusion.1.w_ref, f32[128,256]{1,0:T(8,128)S(1)} %broadcast_multiply_fusion.mask_ref), custom_call_target="tpu_custom_call" | custom-call | tf_op jit(solution)/shard_map/pallas_call | solution.py:44
  16.7 0.0 copy-start.2
  16.7 7.5 %all-to-all-start = ((bf16[128,32,256]{2,1,0:T(8,128)(2,1)}), bf16[128,32,256]{2,1,0:T(8,128)(2,1)S(1)}, u32[]{:S(2)}, u32[]{:S(2)}) async-start(bf16[128,32,256]{2,1,0:T(8,128)(2,1)} %shard_map.73), calls=%async_computation | async-start | bytes 4194304 | tf_op jit(solution)/shard_map/all_to_all | solution.py:165
  24.2 0.0 all-gather.3.cloned.1.call-start
  24.3 0.0 copy-done.2
  24.3 0.1 copy.12
  24.4 26.4 %shard_map.74 = bf16[128,128,256]{2,1,0:T(8,128)(2,1)} custom-call(bf16[128,256,128]{2,1,0:T(8,128)(2,1)} %x_ref.3, bf16[256,128]{1,0:T(8,128)(2,1)S(1)} %multiply_bitcast_fusion.w_ref, f32[128,256]{1,0:T(8,128)S(1)} %broadcast_multiply_fusion.mask_ref), custom_call_target="tpu_custom_call" | custom-call | tf_op jit(solution)/shard_map/pallas_call | solution.py:44
  50.9 1.4 all-to-all-done
  52.2 0.0 copy-start.1
  52.2 1.3 copy-done.1
  53.5 0.0 all-gather.3.cloned.1.call-update
  53.6 104.3 %all_to_all.15 = bf16[128,128,256]{2,1,0:T(8,128)(2,1)} all-to-all(bf16[128,128,256]{2,1,0:T(8,128)(2,1)} %shard_map.74), channel_id=1, replica_groups=mesh['z'=4,'x_lo'=2,'core'=2,'x_hi'=2,'y'=4] {'x_lo','core','x_hi','y'}, dimensions={0} | all-to-all | bytes 16777216 | tf_op jit(solution)/shard_map/all_to_all | solution.py:165
  157.9 0.0 all-gather.3.cloned.1.call-done
  157.9 9.8 %shard_map.75 = bf16[4,8,4,64,128]{4,3,2,1,0:T(8,128)(2,1)} custom-call(bf16[4,8,4,128,256]{4,3,2,1,0:T(8,128)(2,1)} %bitcast.13, bf16[4,4,8,4,32,256]{5,4,3,2,1,0:T(8,128)(2,1)} %bitcast.14), custom_call_target="tpu_custom_call" | custom-call | tf_op jit(solution)/shard_map/pallas_call | solution.py:112
  167.7 0.0 copy-start.4
  167.7 0.0 copy-start.3
  167.7 4.9 %all-to-all-start.2 = ((bf16[128,64,128]{2,1,0:T(8,128)(2,1)}), bf16[128,64,128]{2,1,0:T(8,128)(2,1)}, u32[]{:S(2)}, u32[]{:S(2)}) async-start(bf16[128,64,128]{2,1,0:T(8,128)(2,1)} %bitcast.4), calls=%async_computation.2 | async-start | bytes 4194304 | tf_op jit(solution)/shard_map/all_to_all | solution.py:165
  172.6 0.0 copy-done.4
  172.6 0.1 copy.13.gain_ref
  172.7 0.0 copy-done.3
  172.8 0.0 copy-start
  172.8 4.3 %shard_map.76 = bf16[128,64,128]{2,1,0:T(8,128)(2,1)S(1)} custom-call(bf16[128,2,128,128]{3,2,1,0:T(8,128)(2,1)} %bitcast.12, bf16[128,128]{1,0:T(8,128)(2,1)S(1)} %broadcast_multiply_fusion.1.w_ref), custom_call_target="tpu_custom_call" | custom-call | tf_op jit(solution)/shard_map/pallas_call | solution.py:70
  177.1 23.4 %all-to-all-done.2.p_ref = bf16[128,64,128]{2,1,0:T(8,128)(2,1)} async-done(((bf16[128,64,128]{2,1,0:T(8,128)(2,1)}), bf16[128,64,128]{2,1,0:T(8,128)(2,1)}, u32[]{:S(2)}, u32[]{:S(2)}) %all-to-all-start.2) | async-done | bytes 2097184 | tf_op jit(solution)/shard_map/all_to_all | solution.py:165
  200.5 0.0 copy-done
  200.5 6.7 %shard_map.77 = bf16[2,64,64,128]{3,2,1,0:T(8,128)(2,1)} custom-call(bf16[128,64,128]{2,1,0:T(8,128)(2,1)} %all-to-all-done.2.p_ref, f32[128,1]{1,0:T(8,128)S(1)} %copy.13.gain_ref, bf16[128,128]{1,0:T(8,128)(2,1)S(1)} %copy-done, bf16[2,64,64,128]{3,2,1,0:T(8,128)(2,1)S(1)} %bitcast.11), custom_call_target="tpu_custom_call" | custom-call | tf_op jit(solution)/shard_map/pallas_call | solution.py:147
  (3 shorter events, 0.0 us)
Async XLA Ops:
  16.7 7.6 %copy-start.2 = (bf16[128,256]{1,0:T(8,128)(2,1)S(1)}, bf16[128,256]{1,0:T(8,128)(2,1)}, u32[]{:S(2)}) copy-start(bf16[128,256]{1,0:T(8,128)(2,1)} %param.9) | copy-start | bytes 196612
  16.7 35.5 %all-to-all-start = ((bf16[128,32,256]{2,1,0:T(8,128)(2,1)}), bf16[128,32,256]{2,1,0:T(8,128)(2,1)S(1)}, u32[]{:S(2)}, u32[]{:S(2)}) async-start(bf16[128,32,256]{2,1,0:T(8,128)(2,1)} %shard_map.73), calls=%async_computation | async-start | bytes 4194304 | tf_op jit(solution)/shard_map/all_to_all | solution.py:165
  24.2 133.7 %all-gather.3.cloned.1.call-start = ((), (), s32[]{:S(2)}) async-start(), calls=%async_computation.3 | async-start | bytes 10485760 | tf_op jit(solution)/shard_map/all_gather | solution.py:177
  52.2 1.3 copy-start.1
  167.7 4.9 %copy-start.4 = (f32[128]{0:T(128)S(1)}, f32[128]{0:T(128)}, u32[]{:S(2)}) copy-start(f32[128]{0:T(128)} %param.13) | copy-start | bytes 1540
  167.7 5.0 %copy-start.3 = (bf16[128,128]{1,0:T(8,128)(2,1)S(1)}, bf16[128,128]{1,0:T(8,128)(2,1)}, u32[]{:S(2)}) copy-start(bf16[128,128]{1,0:T(8,128)(2,1)} %param.11) | copy-start | bytes 98308
  167.7 32.8 %all-to-all-start.2 = ((bf16[128,64,128]{2,1,0:T(8,128)(2,1)}), bf16[128,64,128]{2,1,0:T(8,128)(2,1)}, u32[]{:S(2)}, u32[]{:S(2)}) async-start(bf16[128,64,128]{2,1,0:T(8,128)(2,1)} %bitcast.4), calls=%async_computation.2 | async-start | bytes 4194304 | tf_op jit(solution)/shard_map/all_to_all | solution.py:165
  172.8 27.7 %copy-start = (bf16[128,128]{1,0:T(8,128)(2,1)S(1)}, bf16[128,128]{1,0:T(8,128)(2,1)}, u32[]{:S(2)}) copy-start(bf16[128,128]{1,0:T(8,128)(2,1)} %w_ref.1) | copy-start | bytes 98308
Sparse Core Ops, SparseCore 0:
  53.7 84.4 all-gather.2

commit v3 on v1

--- a/solution.py
+++ b/solution.py
@@ -7,6 +7,7 @@
 from jax.experimental.pallas import tpu as pltpu
 from jax.sharding import PartitionSpec as P
 
+TOK_ROW = 128
 WIN_BLK = 32
 ROW_STEP = 16
 AXES = ("row", "chan")
@@ -23,43 +24,56 @@
     return (centred * lax.rsqrt(var + 1e-05)).astype(jnp.bfloat16)
 
 
-def project_kernel(x_ref, w_ref, mask_ref, o_ref, swap):
+def project_kernel(first, tok_s_ref, tok_v_ref, x_ref, w_ref, o_ref, w_swap, swap):
     rows, cols, chans = x_ref.shape
+    pitch = chans + 1
+
+    @pl.when(pl.program_id(0) == 0)
+    def _():
+        w_swap[...] = (0.5 * w_ref[...].astype(jnp.float32)).T.astype(jnp.bfloat16)
+
+    own_row = lax.axis_index("row") * TOK_ROW + first + pl.program_id(0) * rows
+    own_col = lax.axis_index("chan") * (cols // 128)
+    col_mask = [tok_v_ref[pl.ds(own_col + h, 1), :].astype(jnp.float32) for h in range(cols // 128)]
     normed = normed_rows(x_ref[...].reshape(rows * cols, chans))
     for i in range(rows):
-        both = lax.dot_general(w_ref[...], normed[i * cols:(i + 1) * cols], NT, preferred_element_type=jnp.float32)
-        gated = (jnp.tanh(both[:chans]) + 1.0) * both[chans:] * mask_ref[i:i + 1, :]
+        both = lax.dot_general(w_swap[...], normed[i * cols:(i + 1) * cols], NT, preferred_element_type=jnp.float32)
+        gated = (jnp.tanh(both[:chans]) + 1.0) * both[chans:]
+        row_mask = tok_s_ref[own_row + i].astype(jnp.float32)
         for h in range(cols // 128):
-            swap[h, i * chans:(i + 1) * chans, :] = gated[:, h * 128:(h + 1) * 128]
+            swap[h, i * pitch:i * pitch + chans, :] = gated[:, h * 128:(h + 1) * 128] * (col_mask[h] * row_mask)
     for c in range(chans):
         for h in range(cols // 128):
-            o_ref[c, :, h * 128:(h + 1) * 128] = swap[h, pl.ds(c, rows, stride=chans), :].astype(jnp.bfloat16)
+            o_ref[c, :, h * 128:(h + 1) * 128] = swap[h, pl.ds(c, rows, stride=pitch), :].astype(jnp.bfloat16)
 
 
-def project(pair, weight, mask, first, rows):
+def project(pair, weight, token_mask, first, rows):
     cols, chans = pair.shape[1:]
-    weight = (0.5 * weight.T).astype(jnp.bfloat16)
     base = first // ROW_STEP
     return pl.pallas_call(
-        project_kernel,
+        functools.partial(project_kernel, first),
         grid=(rows // ROW_STEP,),
         in_specs=[
+            pl.BlockSpec(memory_space=pltpu.SMEM),
+            pl.BlockSpec((token_mask.shape[0] // 128, 128), lambda s: (0, 0)),
             pl.BlockSpec((ROW_STEP, cols, chans), lambda s: (base + s, 0, 0)),
-            pl.BlockSpec((2 * chans, chans), lambda s: (0, 0)),
-            pl.BlockSpec((ROW_STEP, cols), lambda s: (base + s, 0)),
+            pl.BlockSpec((chans, 2 * chans), lambda s: (0, 0)),
         ],
         out_specs=pl.BlockSpec((chans, ROW_STEP, cols), lambda s: (0, s, 0)),
         out_shape=jax.ShapeDtypeStruct((chans, rows, cols), jnp.bfloat16),
-        scratch_shapes=[pltpu.VMEM((cols // 128, ROW_STEP * chans, 128), jnp.float32)],
+        scratch_shapes=[
+            pltpu.VMEM((2 * chans, chans), jnp.bfloat16),
+            pltpu.VMEM((cols // 128, ROW_STEP * (chans + 1), 128), jnp.float32),
+        ],
         compiler_params=pltpu.CompilerParams(vmem_limit_bytes=48 << 20),
-    )(pair, weight, mask)
+    )(token_mask, token_mask.reshape(-1, 128), pair, weight)
 
 
 def gate_kernel(x_ref, w_ref, o_ref):
-    rows, blks, blk, _, chans = x_ref.shape[0], x_ref.shape[1], WIN_BLK, 0, x_ref.shape[-1]
+    rows, blks, blk, chans = x_ref.shape
     normed = normed_rows(x_ref[...].reshape(rows * blks * blk, chans))
     gate = jnp.dot(normed, w_ref[...], preferred_element_type=jnp.float32)
-    o_ref[...] = (0.5 * jnp.tanh(gate) + 0.5).reshape(rows, blks * blk, chans).astype(jnp.bfloat16)
+    o_ref[...] = (0.5 * jnp.tanh(0.5 * gate) + 0.5).reshape(rows, blks * blk, chans).astype(jnp.bfloat16)
 
 
 def gate_of(pair, w_gate):
@@ -76,7 +90,7 @@
         out_specs=pl.BlockSpec((32, blks * WIN_BLK, chans), lambda s: (s, 0, 0)),
         out_shape=jax.ShapeDtypeStruct((rows, blks * WIN_BLK, chans), jnp.bfloat16),
         compiler_params=pltpu.CompilerParams(vmem_limit_bytes=48 << 20),
-    )(blocks, (0.5 * w_gate).astype(jnp.bfloat16))
+    )(blocks, w_gate)
 
 
 def product_kernel(a_ref, b_ref, o_ref, acc):
@@ -121,16 +135,19 @@
     return out.reshape(n_row * n_chan, rows // 2, 128)
 
 
-def finish_kernel(p_ref, gain_ref, w_ref, gate_ref, o_ref, swap):
+def finish_kernel(gain_ref, p_ref, w_ref, gate_ref, o_ref, swap):
     chans, subs, lanes = p_ref.shape
+    pitch = subs + 1
     x = p_ref[...].astype(jnp.float32)
     mean = jnp.sum(x, axis=0) * (1.0 / chans)
     centred = x - mean[None]
     var = jnp.sum(centred * centred, axis=0) * (1.0 / chans)
-    swap[...] = (centred * lax.rsqrt(var + 1e-05)[None]).reshape(chans * subs, lanes)
+    scale = lax.rsqrt(var + 1e-05)
+    for c in range(chans):
+        swap[c * pitch:c * pitch + subs, :] = centred[c] * scale * gain_ref[c]
     half = lanes // 2
     for s in range(subs):
-        normed = (swap[pl.ds(s, chans, stride=subs), :] * gain_ref[...]).astype(jnp.bfloat16)
+        normed = swap[pl.ds(s, chans, stride=pitch), :].astype(jnp.bfloat16)
         outcome = lax.dot_general(normed, w_ref[...], TN, preferred_element_type=jnp.float32)
         for h in range(2):
             gate = gate_ref[h, s].astype(jnp.float32)
@@ -145,16 +162,16 @@
         finish_kernel,
         grid=(subs // step,),
         in_specs=[
+            pl.BlockSpec(memory_space=pltpu.SMEM),
             pl.BlockSpec((chans, step, lanes), lambda s: (0, s, 0)),
-            pl.BlockSpec((chans, 1), lambda s: (0, 0)),
             pl.BlockSpec((chans, chans), lambda s: (0, 0)),
             pl.BlockSpec((2, step, wins, chans), lambda s: (0, s, 0, 0)),
         ],
         out_specs=pl.BlockSpec((2, step, wins, chans), lambda s: (0, s, 0, 0)),
         out_shape=jax.ShapeDtypeStruct((2, subs, wins, chans), jnp.bfloat16),
-        scratch_shapes=[pltpu.VMEM((chans * step, lanes), jnp.float32)],
+        scratch_shapes=[pltpu.VMEM((chans * (step + 1), lanes), jnp.float32)],
         compiler_params=pltpu.CompilerParams(vmem_limit_bytes=48 << 20),
-    )(product, out_gain.reshape(chans, 1), w_out, gate.reshape(2, subs, wins, chans))
+    )(out_gain, product, w_out, gate.reshape(2, subs, wins, chans))
     return out.reshape(rows, wins, chans)
 
 
@@ -163,13 +180,8 @@
 
 
 def per_device(n_row, n_chan, pair, token_mask, w_left, w_right, w_gate, w_out, out_gain):
-    tok_rows, columns, chans = pair.shape
-    maskf = token_mask.astype(jnp.float32)
-    row_mask = lax.dynamic_slice_in_dim(maskf, lax.axis_index("row") * tok_rows, tok_rows, 0)
-    col_mask = lax.dynamic_slice_in_dim(maskf, lax.axis_index("chan") * columns, columns, 0)
-    mask = row_mask[:, None] * col_mask[None, :]
-    right = spread(project(pair, w_right, mask, 0, WIN_BLK))
-    left = spread(project(pair, w_left, mask, 0, tok_rows))
+    right = spread(project(pair, w_right, token_mask, 0, WIN_BLK))
+    left = spread(project(pair, w_left, token_mask, 0, pair.shape[0]))
     gate = gate_of(pair, w_gate)
     product = spread(product_of(left, right, n_row, n_chan))
     return finish(product, out_gain, w_out, gate)

time: 208 us -> 203 us (0.976)
  Pallas kernels: 52.3 us -> 37.4 us
  waiting for transfers between devices: 28.8 us -> 40.7 us
    pallas_call x2, Pallas kernels: 33.9 us -> 20.2 us  [project(): pl.pallas_call(functools.partial(project_kernel, first), grid=(rows // RO...]
    all_to_all x2, waiting for transfers between devices: 28.8 us -> 40.7 us  [spread(): return lax.all_to_all(values, AXES, split_axis=0, concat_axis=0, tiled=True)]
  transfers between devices with their start and end apart: 2 -> 2, of which waited for: 2 -> 2; matrix products, arithmetic and copies ran while one was open for 0% -> 0% of each run, Pallas kernels for 15% -> 9%
where the time goes in v3:
time: 203 us; the launch traced here: 202 us
  blocking collectives  103 us (51%)
  waiting for transfers between devices  40.7 us (20%)
  Pallas kernels  37.4 us (18%)
  starting transfers between devices  17.6 us (9%)
  local copies, waits for them, and re-layouts  2.87 us (1%)
    all_to_all x1, blocking collectives, spread(): return lax.all_to_all(values, AXES, split_axis=0, concat_axis=0, tiled=True)  103 us
    all_to_all x2, waiting for transfers between devices, spread(): return lax.all_to_all(values, AXES, split_axis=0, concat_axis=0, tiled=True)  40.7 us
    pallas_call x2, Pallas kernels, project(): pl.pallas_call(functools.partial(project_kernel, first), grid=(rows // RO...  20.2 us
    all_to_all x2, starting transfers between devices, spread(): return lax.all_to_all(values, AXES, split_axis=0, concat_axis=0, tiled=True)  17.6 us
    pallas_call x1, Pallas kernels, product_of(): pl.pallas_call(product_kernel, grid=(n_row // steps,), in_specs=[pl.Block...  7.35 us
    pallas_call x1, Pallas kernels, finish(): pl.pallas_call(finish_kernel, grid=(subs // step,), in_specs=[pl.BlockSpe...  5.56 us
    pallas_call x1, Pallas kernels, gate_of(): pl.pallas_call(gate_kernel, grid=(rows // 32,), in_specs=[pl.BlockSpec((3...  4.29 us
  transfers between devices with their start and end apart: 2, of which 2 were waited for; matrix products, arithmetic and copies ran while one was open for 0% of the time, Pallas kernels for 9%

profile of v3, /device:TPU:0, one launch (start us, length us, event | category | flops | bytes accessed | tf_op | source)
XLA Modules:
  0.0 201.9 jit_solution(5004972250803840122)
XLA Ops:
  0.0 0.0 copy-start.1
  0.0 0.7 copy-done.1
  0.7 0.0 copy-start.3
  0.7 0.8 copy-done.3
  1.5 5.3 %shard_map.74 = bf16[128,32,256]{2,1,0:T(8,128)(2,1)} custom-call(s32[2048]{0:T(1024)S(1)} %copy-done.1, s32[16,128]{1,0:T(8,128)S(1)} %bitcast.10, bf16[128,256,128]{2,1,0:T(8,128)(2,1)} %x_ref.3, bf16[128,256]{1,0:T(8,128)(2,1)S(1)} %copy-done.3), custom_call_target="tpu_custom_call" | custom-call | tf_op jit(solution)/shard_map/pallas_call | solution.py:53
  6.9 0.0 copy-start.2
  6.9 0.0 copy-start.4
  6.9 11.1 %all-to-all-start.1 = ((bf16[128,32,256]{2,1,0:T(8,128)(2,1)}), bf16[128,32,256]{2,1,0:T(8,128)(2,1)S(1)}, u32[]{:S(2)}, u32[]{:S(2)}) async-start(bf16[128,32,256]{2,1,0:T(8,128)(2,1)} %shard_map.74), calls=%async_computation.1 | async-start | bytes 4194304 | tf_op jit(solution)/shard_map/all_to_all | solution.py:179
  18.0 0.0 copy-done.2
  18.0 0.0 copy-done.4
  18.1 14.9 %shard_map.73 = bf16[128,128,256]{2,1,0:T(8,128)(2,1)} custom-call(s32[2048]{0:T(1024)S(1)} %copy-done.2, s32[16,128]{1,0:T(8,128)S(1)} %bitcast.11, bf16[128,256,128]{2,1,0:T(8,128)(2,1)} %x_ref.3, bf16[128,256]{1,0:T(8,128)(2,1)S(1)} %copy-done.4), custom_call_target="tpu_custom_call" | custom-call | tf_op jit(solution)/shard_map/pallas_call | solution.py:53
  32.9 15.3 %all-to-all-done.1 = bf16[128,32,256]{2,1,0:T(8,128)(2,1)S(1)} async-done(((bf16[128,32,256]{2,1,0:T(8,128)(2,1)}), bf16[128,32,256]{2,1,0:T(8,128)(2,1)S(1)}, u32[]{:S(2)}, u32[]{:S(2)}) %all-to-all-start.1) | async-done | bytes 2097184 | tf_op jit(solution)/shard_map/all_to_all | solution.py:179
  48.2 103.3 %all_to_all.15 = bf16[128,128,256]{2,1,0:T(8,128)(2,1)} all-to-all(bf16[128,128,256]{2,1,0:T(8,128)(2,1)} %shard_map.73), channel_id=1, replica_groups=mesh['row'=16,'chan'=8] {'row','chan'}, dimensions={0} | all-to-all | bytes 16777216 | tf_op jit(solution)/shard_map/all_to_all | solution.py:179
  151.5 7.3 %shard_map.75 = bf16[16,8,64,128]{3,2,1,0:T(8,128)(2,1)S(1)} custom-call(bf16[16,8,128,256]{3,2,1,0:T(8,128)(2,1)} %bitcast.13, bf16[16,8,32,256]{3,2,1,0:T(8,128)(2,1)S(1)} %bitcast.8), custom_call_target="tpu_custom_call" | custom-call | tf_op jit(solution)/shard_map/pallas_call | solution.py:123
  158.8 0.0 copy-start
  158.9 1.3 copy-done
  160.2 0.0 copy-start.5
  160.2 6.4 %all-to-all-start.2 = ((bf16[128,64,128]{2,1,0:T(8,128)(2,1)}), bf16[128,64,128]{2,1,0:T(8,128)(2,1)}, u32[]{:S(2)}, u32[]{:S(2)}) async-start(bf16[128,64,128]{2,1,0:T(8,128)(2,1)} %bitcast.9), calls=%async_computation.2 | async-start | bytes 4194304 | tf_op jit(solution)/shard_map/all_to_all | solution.py:179
  166.6 0.0 copy-done.5
  166.6 0.0 copy-start.6
  166.6 0.0 copy-start.7
  166.6 4.3 %shard_map.76 = bf16[128,64,128]{2,1,0:T(8,128)(2,1)S(1)} custom-call(bf16[128,2,128,128]{3,2,1,0:T(8,128)(2,1)} %bitcast.12, bf16[128,128]{1,0:T(8,128)(2,1)S(1)} %copy-done.5), custom_call_target="tpu_custom_call" | custom-call | tf_op jit(solution)/shard_map/pallas_call | solution.py:83
  170.9 25.4 %all-to-all-done.2.p_ref = bf16[128,64,128]{2,1,0:T(8,128)(2,1)} async-done(((bf16[128,64,128]{2,1,0:T(8,128)(2,1)}), bf16[128,64,128]{2,1,0:T(8,128)(2,1)}, u32[]{:S(2)}, u32[]{:S(2)}) %all-to-all-start.2) | async-done | bytes 2097184 | tf_op jit(solution)/shard_map/all_to_all | solution.py:179
  196.4 0.0 copy-done.6
  196.4 0.0 copy-done.7
  196.4 5.6 %shard_map.77 = bf16[2,64,64,128]{3,2,1,0:T(8,128)(2,1)} custom-call(f32[128]{0:T(128)S(1)} %copy-done.7, bf16[128,64,128]{2,1,0:T(8,128)(2,1)} %all-to-all-done.2.p_ref, bf16[128,128]{1,0:T(8,128)(2,1)S(1)} %copy-done.6, bf16[2,64,64,128]{3,2,1,0:T(8,128)(2,1)S(1)} %bitcast.7), custom_call_target="tpu_custom_call" | custom-call | tf_op jit(solution)/shard_map/pallas_call | solution.py:161
Async XLA Ops:
  0.0 0.7 copy-start.1
  0.7 0.8 copy-start.3
  6.9 11.2 %copy-start.2 = (s32[2048]{0:T(1024)S(1)}, s32[2048]{0:T(1024)}, u32[]{:S(2)}) copy-start(s32[2048]{0:T(1024)} %tok_s_ref.3) | copy-start | bytes 24580
  6.9 11.2 %copy-start.4 = (bf16[128,256]{1,0:T(8,128)(2,1)S(1)}, bf16[128,256]{1,0:T(8,128)(2,1)}, u32[]{:S(2)}) copy-start(bf16[128,256]{1,0:T(8,128)(2,1)} %w_ref.4) | copy-start | bytes 196612
  6.9 41.3 %all-to-all-start.1 = ((bf16[128,32,256]{2,1,0:T(8,128)(2,1)}), bf16[128,32,256]{2,1,0:T(8,128)(2,1)S(1)}, u32[]{:S(2)}, u32[]{:S(2)}) async-start(bf16[128,32,256]{2,1,0:T(8,128)(2,1)} %shard_map.74), calls=%async_computation.1 | async-start | bytes 4194304 | tf_op jit(solution)/shard_map/all_to_all | solution.py:179
  158.8 1.3 copy-start
  160.2 6.4 %copy-start.5 = (bf16[128,128]{1,0:T(8,128)(2,1)S(1)}, bf16[128,128]{1,0:T(8,128)(2,1)}, u32[]{:S(2)}) copy-start(bf16[128,128]{1,0:T(8,128)(2,1)} %w_ref.6) | copy-start | bytes 98308
  160.2 36.2 %all-to-all-start.2 = ((bf16[128,64,128]{2,1,0:T(8,128)(2,1)}), bf16[128,64,128]{2,1,0:T(8,128)(2,1)}, u32[]{:S(2)}, u32[]{:S(2)}) async-start(bf16[128,64,128]{2,1,0:T(8,128)(2,1)} %bitcast.9), calls=%async_computation.2 | async-start | bytes 4194304 | tf_op jit(solution)/shard_map/all_to_all | solution.py:179
  166.6 29.7 %copy-start.6 = (bf16[128,128]{1,0:T(8,128)(2,1)S(1)}, bf16[128,128]{1,0:T(8,128)(2,1)}, u32[]{:S(2)}) copy-start(bf16[128,128]{1,0:T(8,128)(2,1)} %w_ref.7) | copy-start | bytes 98308
  166.6 29.7 %copy-start.7 = (f32[128]{0:T(128)S(1)}, f32[128]{0:T(128)}, u32[]{:S(2)}) copy-start(f32[128]{0:T(128)} %gain_ref.1) | copy-start | bytes 1540

commit v4 on v1

v4 whole, which is shorter than its diff:
```python
import jax
import jax.numpy as jnp
from jax import lax
from jax.experimental import pallas as pl
from jax.experimental.pallas import tpu as pltpu
from jax.sharding import PartitionSpec as P

TOK_ROW = 128
WIN_BLK = 32
ROW_STEP = 16
PROJECT_VMEM = 48 << 20
AXES = ("row", "chan")
NT = (((1,), (1,)), ((), ()))
TN = (((0,), (0,)), ((), ()))


def normed_rows(x):
    chans = x.shape[-1]
    avg = jnp.full((chans, chans), 1.0 / chans, jnp.bfloat16)
    mean = jnp.dot(x, avg, preferred_element_type=jnp.float32)
    centred = x.astype(jnp.float32) - mean
    var = jnp.dot((centred * centred).astype(jnp.bfloat16), avg, preferred_element_type=jnp.float32)
    return (centred * lax.rsqrt(var + 1e-05)).astype(jnp.bfloat16)


def project_kernel(x_ref, left_ref, right_ref, tok_ref, o_ref, weights, swap):
    rows, cols, chans = x_ref.shape
    pitch = chans + 1
    step = pl.program_id(0)
    wins = WIN_BLK // rows

    @pl.when(step == 0)
    def _():
        weights[:2 * chans] = (0.5 * left_ref[...].astype(jnp.float32)).T.astype(jnp.bfloat16)
        weights[2 * chans:] = (0.5 * right_ref[...].astype(jnp.float32)).T.astype(jnp.bfloat16)

    own_col = lax.axis_index("chan") * (cols // 128)
    mask = jnp.concatenate([tok_ref[pl.ds(own_col + h, 1), :] for h in range(cols // 128)], axis=1).astype(jnp.float32)

    def sides(count):
        for i in range(rows):
            x = x_ref[i].T.astype(jnp.float32)
            centred = x - jnp.mean(x, axis=0, keepdims=True)
            var = jnp.mean(centred * centred, axis=0, keepdims=True)
            normed = (centred * (lax.rsqrt(var + 1e-05) * mask)).astype(jnp.bfloat16)
            both = jnp.dot(weights[:2 * chans * count], normed, preferred_element_type=jnp.float32)
            for side in range(count):
                gate, value = both[2 * side * chans:(2 * side + 1) * chans], both[(2 * side + 1) * chans:2 * (side + 1) * chans]
                gated = (jnp.tanh(gate) + 1.0) * value
                for h in range(cols // 128):
                    swap[side, h, i * pitch:i * pitch + chans, :] = gated[:, h * 128:(h + 1) * 128]
        for side in range(count):
            at = pl.multiple_of(step * rows + (0 if side else WIN_BLK), rows)
            for c in range(chans):
                for h in range(cols // 128):
                    o_ref[c, pl.ds(at, rows), h * 128:(h + 1) * 128] = (
                        swap[side, h, pl.ds(c, rows, stride=pitch), :].astype(jnp.bfloat16))

    pl.when(step < wins)(lambda: sides(2))
    pl.when(step >= wins)(lambda: sides(1))


def project(pair, w_left, w_right, token_mask):
    rows, cols, chans = pair.shape
    tokens = token_mask.reshape(-1, 128)
    return pl.pallas_call(
        project_kernel,
        grid=(rows // ROW_STEP,),
        in_specs=[
            pl.BlockSpec((ROW_STEP, cols, chans), lambda s: (s, 0, 0)),
            pl.BlockSpec((chans, 2 * chans), lambda s: (0, 0)),
            pl.BlockSpec((chans, 2 * chans), lambda s: (0, 0)),
            pl.BlockSpec(tokens.shape, lambda s: (0, 0)),
        ],
        out_specs=pl.BlockSpec(memory_space=pltpu.VMEM),
        out_shape=pltpu.VMEM((chans, WIN_BLK + rows, cols), jnp.bfloat16),
        scratch_shapes=[
            pltpu.VMEM((4 * chans, chans), jnp.bfloat16),
            pltpu.VMEM((2, cols // 128, ROW_STEP * (chans + 1), 128), jnp.float32),
        ],
        compiler_params=pltpu.CompilerParams(vmem_limit_bytes=PROJECT_VMEM),
    )(pair, w_left, w_right, tokens)


def gate_kernel(tok_ref, x_ref, w_ref, o_ref, mask):
    rows, blks, blk, chans = x_ref.shape

    @pl.when(pl.program_id(0) == 0)
    def _():
        for h in range(blks):
            own_col = (lax.axis_index("chan") * blks + h) * 128
            for t in range(blk):
                mask[h * blk + t:h * blk + t + 1, :] = jnp.full((1, chans), tok_ref[own_col + t].astype(jnp.float32))

    own_row = lax.axis_index("row") * TOK_ROW + pl.program_id(0) * rows
    normed = normed_rows(x_ref[...].reshape(rows * blks * blk, chans))
    gate = jnp.dot(normed, w_ref[...], preferred_element_type=jnp.float32)
    gate = (0.5 * jnp.tanh(0.5 * gate) + 0.5).reshape(rows, blks * blk, chans)
    for i in range(rows):
        o_ref[i] = (gate[i] * (mask[...] * tok_ref[own_row + i].astype(jnp.float32))).astype(jnp.bfloat16)


def gate_of(pair, w_gate, token_mask):
    rows, cols, chans = pair.shape
    blks = cols // 128
    blocks = pair.reshape(rows, blks, 128, chans)
    return pl.pallas_call(
        gate_kernel,
        grid=(rows // 32,),
        in_specs=[
            pl.BlockSpec(memory_space=pltpu.SMEM),
            pl.BlockSpec((32, blks, WIN_BLK, chans), lambda s: (s, 0, 0, 0)),
            pl.BlockSpec((chans, chans), lambda s: (0, 0)),
        ],
        out_specs=pl.BlockSpec((None, 32, blks * WIN_BLK, chans), lambda s: (s // 2, s % 2, 0, 0)),
        out_shape=pltpu.HBM((2, rows // 2, blks * WIN_BLK, chans), jnp.bfloat16),
        scratch_shapes=[pltpu.VMEM((blks * WIN_BLK, chans), jnp.float32)],
        compiler_params=pltpu.CompilerParams(vmem_limit_bytes=20 << 20),
    )(token_mask, blocks, w_gate)


def product_kernel(x_ref, o_hbm, acc, out, sem):
    n_row, n_chan, rows, depth = x_ref.shape
    rows -= WIN_BLK
    wins = n_row * WIN_BLK
    steps = acc.shape[0] // rows
    half = rows // 2
    low = lax.broadcasted_iota(jnp.int32, (half, 128), 1) < 64
    copies = []
    for first in range(0, n_row, steps):
        for q in range(n_chan):
            term = lax.dot_general(
                x_ref[first:first + steps, q, WIN_BLK:].reshape(steps * rows, depth),
                x_ref[:, q, :WIN_BLK].reshape(wins, depth), NT, preferred_element_type=jnp.float32)
            if q == 0:
                acc[...] = term
            else:
                acc[...] += term
        for r in range(steps):
            for m in range(wins // 128):
                top = acc[r * rows:r * rows + half, m * 128:(m + 1) * 128]
                bot = acc[r * rows + half:(r + 1) * rows, m * 128:(m + 1) * 128]
                out[first + r, 2 * m] = jnp.where(low, top, pltpu.roll(bot, 64, 1)).astype(jnp.bfloat16)
                out[first + r, 2 * m + 1] = jnp.where(low, pltpu.roll(top, 64, 1), bot).astype(jnp.bfloat16)
        part = pl.ds(first, steps)
        copies.append(pltpu.make_async_copy(out.at[part], o_hbm.at[part], sem.at[first // steps]))
        copies[-1].start()
    for copy in copies:
        copy.wait()


def product_of(sides):
    n_row, n_chan = lax.axis_size("row"), lax.axis_size("chan")
    _, rows, depth = sides.shape
    half = (rows - WIN_BLK) // 2
    shape = (n_row, n_chan, half, 128)
    steps = 4
    out = pl.pallas_call(
        product_kernel,
        in_specs=[pl.BlockSpec(memory_space=pltpu.VMEM)],
        out_specs=pl.BlockSpec(memory_space=pltpu.HBM),
        out_shape=pltpu.HBM(shape, jnp.bfloat16),
        scratch_shapes=[
            pltpu.VMEM((steps * 2 * half, n_row * WIN_BLK), jnp.float32),
            pltpu.VMEM(shape, jnp.bfloat16),
            pltpu.SemaphoreType.DMA((n_row // steps,)),
        ],
        compiler_params=pltpu.CompilerParams(vmem_limit_bytes=16 << 20),
    )(sides.reshape(n_row, n_chan, rows, depth))
    return out.reshape(n_row * n_chan, half, 128)


def finish_kernel(gain_ref, p_ref, w_ref, gate_hbm, o_ref, swap, gate_ref, sem):
    chans, subs, lanes = p_ref.shape
    pitch = subs + 1
    half = lanes // 2
    step = pl.program_id(0)

    def gate_copy(n):
        part = pl.ds(pl.multiple_of(n * subs, subs), subs)
        return pltpu.make_async_copy(gate_hbm.at[:, part], gate_ref.at[n], sem.at[n])

    @pl.when(step == 0)
    def _():
        for n in range(gate_ref.shape[0]):
            gate_copy(n).start()

    x = p_ref[...].astype(jnp.float32)
    mean = jnp.sum(x, axis=0) * (1.0 / chans)
    centred = x - mean[None]
    var = jnp.sum(centred * centred, axis=0) * (1.0 / chans)
    scale = lax.rsqrt(var + 1e-05)
    for c in range(chans):
        swap[c * pitch:c * pitch + subs, :] = centred[c] * scale * gain_ref[c]
    gate_copy(step).wait()
    for s in range(subs):
        normed = swap[pl.ds(s, chans, stride=pitch), :].astype(jnp.bfloat16)
        outcome = lax.dot_general(normed, w_ref[...], TN, preferred_element_type=jnp.float32)
        for h in range(2):
            gate = gate_ref[step, h, s].astype(jnp.float32)
            o_ref[h, s] = (gate * outcome[h * half:(h + 1) * half]).astype(jnp.bfloat16)


def finish(product, out_gain, w_out, gate):
    chans, subs, lanes = product.shape
    rows, wins = 2 * subs, gate.shape[2]
    step = 16
    out = pl.pallas_call(
        finish_kernel,
        grid=(subs // step,),
        in_specs=[
            pl.BlockSpec(memory_space=pltpu.SMEM),
            pl.BlockSpec((chans, step, lanes), lambda s: (0, s, 0)),
            pl.BlockSpec((chans, chans), lambda s: (0, 0)),
            pl.BlockSpec(memory_space=pltpu.HBM),
        ],
        out_specs=pl.BlockSpec((2, step, wins, chans), lambda s: (0, s, 0, 0)),
        out_shape=pltpu.HBM((2, subs, wins, chans), jnp.bfloat16),
        scratch_shapes=[
            pltpu.VMEM((chans * (step + 1), lanes), jnp.float32),
            pltpu.VMEM((subs // step, 2, step, wins, chans), jnp.bfloat16),
            pltpu.SemaphoreType.DMA((subs // step,)),
        ],
        compiler_params=pltpu.CompilerParams(vmem_limit_bytes=60 << 20),
    )(out_gain, product, w_out, gate)
    return out.reshape(rows, wins, chans)


def spread(values):
    return lax.all_to_all(values, AXES, split_axis=0, concat_axis=0, tiled=True)


def per_device(pair, token_mask, w_left, w_right, w_gate, w_out, out_gain):
    sides = spread(project(pair, w_left, w_right, token_mask))
    gate = gate_of(pair, w_gate, token_mask)
    product = spread(product_of(sides))
    return finish(product, out_gain, w_out, gate)


def solution(mesh):
    in_specs = (P("row", "chan", None), P(), P(), P(), P(), P(), P())
    out_specs = P("row", "chan", None)
    return jax.shard_map(
        per_device, mesh=mesh, in_specs=in_specs, out_specs=out_specs, check_vma=False
    )
```

time: 208 us -> 194 us (0.933)
  blocking collectives: 104 us -> 131 us
  Pallas kernels: 52.3 us -> 30 us
  starting transfers between devices: 17.6 us -> 5.6 us
  waiting for transfers between devices: 28.8 us -> 22 us
    all_to_all x1, blocking collectives: 104 us -> 131 us  [spread(): return lax.all_to_all(values, AXES, split_axis=0, concat_axis=0, tiled=True)]
    pallas_call x2 -> x1, Pallas kernels: 33.9 us -> 13.7 us  [project(): pl.pallas_call(project_kernel, grid=(rows // ROW_STEP,), in_specs=[pl.Blo...]
    all_to_all x2 -> x1, starting transfers between devices: 17.6 us -> 5.6 us  [spread(): return lax.all_to_all(values, AXES, split_axis=0, concat_axis=0, tiled=True)]
    all_to_all x2 -> x1, waiting for transfers between devices: 28.8 us -> 22 us  [spread(): return lax.all_to_all(values, AXES, split_axis=0, concat_axis=0, tiled=True)]
    unnamed x14 -> x8, local copies, waits for them, and re-layouts: 3.7 us -> 4.73 us
  transfers between devices with their start and end apart: 2 -> 1, of which waited for: 2 -> 1; matrix products, arithmetic and copies ran while one was open for 0% -> 0% of each run, Pallas kernels for 15% -> 2%
where the time goes in v4:
time: 194 us
  blocking collectives  131 us (68%)
  Pallas kernels  30 us (15%)
  waiting for transfers between devices  22 us (11%)
  starting transfers between devices  5.6 us (3%)
  local copies, waits for them, and re-layouts  4.73 us (2%)
    all_to_all x1, blocking collectives, spread(): return lax.all_to_all(values, AXES, split_axis=0, concat_axis=0, tiled=True)  131 us
    all_to_all x1, waiting for transfers between devices, spread(): return lax.all_to_all(values, AXES, split_axis=0, concat_axis=0, tiled=True)  22 us
    pallas_call x1, Pallas kernels, project(): pl.pallas_call(project_kernel, grid=(rows // ROW_STEP,), in_specs=[pl.Blo...  13.7 us
    pallas_call x1, Pallas kernels, finish(): pl.pallas_call(finish_kernel, grid=(subs // step,), in_specs=[pl.BlockSpe...  6.21 us
    all_to_all x1, starting transfers between devices, spread(): return lax.all_to_all(values, AXES, split_axis=0, concat_axis=0, tiled=True)  5.6 us
    pallas_call x1, Pallas kernels, product_of(): pl.pallas_call(product_kernel, in_specs=[pl.BlockSpec(memory_space=pltpu....  5.43 us
    pallas_call x1, Pallas kernels, gate_of(): pl.pallas_call(gate_kernel, grid=(rows // 32,), in_specs=[pl.BlockSpec(me...  4.74 us
    unnamed x8, local copies, waits for them, and re-layouts  4.73 us
  transfers between devices with their start and end apart: 1, of which 1 were waited for; matrix products, arithmetic and copies ran while one was open for 0% of the time, Pallas kernels for 2%

profile of v4, /device:TPU:0, one launch (start us, length us, event | category | flops | bytes accessed | tf_op | source)
XLA Modules:
  0.0 193.8 jit_solution(15366563885615140317)
XLA Ops:
  0.0 13.7 %shard_map.73 = bf16[128,160,256]{2,1,0:T(8,128)(2,1)S(1)} custom-call(bf16[128,256,128]{2,1,0:T(8,128)(2,1)} %x_ref.1, bf16[128,256]{1,0:T(8,128)(2,1)} %left_ref.1, bf16[128,256]{1,0:T(8,128)(2,1)} %right_ref.1, s32[16,128]{1,0:T(8,128)} %bitcast.7), custom_call_target="tpu_custom_call" | custom-call | tf_op jit(solution)/shard_map/pallas_call | solution.py:66
  13.7 131.3 %all_to_all.10 = bf16[128,160,256]{2,1,0:T(8,128)(2,1)S(1)} all-to-all(bf16[128,160,256]{2,1,0:T(8,128)(2,1)S(1)} %shard_map.73), channel_id=1, replica_groups=mesh['row'=16,'chan'=8] {'row','chan'}, dimensions={0} | all-to-all | bytes 20971520 | tf_op jit(solution)/shard_map/all_to_all | solution.py:230
  145.0 5.4 %shard_map.74 = bf16[16,8,64,128]{3,2,1,0:T(8,128)(2,1)} custom-call(bf16[16,8,160,256]{3,2,1,0:T(8,128)(2,1)S(1)} %bitcast.5), custom_call_target="tpu_custom_call" | custom-call | tf_op jit(solution)/shard_map/pallas_call | solution.py:158
  150.4 0.0 copy-start.1
  150.5 0.0 copy-start.2
  150.5 5.6 %all-to-all-start.1 = ((bf16[128,64,128]{2,1,0:T(8,128)(2,1)}), bf16[128,64,128]{2,1,0:T(8,128)(2,1)S(1)}, u32[]{:S(2)}, u32[]{:S(2)}) async-start(bf16[128,64,128]{2,1,0:T(8,128)(2,1)} %bitcast.8), calls=%async_computation.1 | async-start | bytes 4194304 | tf_op jit(solution)/shard_map/all_to_all | solution.py:230
  156.1 0.0 copy-done.1
  156.1 0.0 copy-done.2
  156.1 0.0 copy-start
  156.1 3.4 %copy-done = bf16[128,256,128]{2,1,0:T(8,128)(2,1)S(1)} copy-done((bf16[128,256,128]{2,1,0:T(8,128)(2,1)S(1)}, bf16[128,256,128]{2,1,0:T(8,128)(2,1)}, u32[]{:S(2)}) %copy-start) | copy-done | bytes 8388632
  159.5 4.7 %shard_map.75.gate_hbm = bf16[2,64,64,128]{3,2,1,0:T(8,128)(2,1)} custom-call(s32[2048]{0:T(1024)S(1)} %copy-done.2, bf16[128,2,128,128]{3,2,1,0:T(8,128)(2,1)S(1)} %bitcast.6, bf16[128,128]{1,0:T(8,128)(2,1)S(1)} %copy-done.1), custom_call_target="tpu_custom_call" | custom-call | tf_op jit(solution)/shard_map/pallas_call | solution.py:107
  164.2 22.0 %all-to-all-done.1.p_ref = bf16[128,64,128]{2,1,0:T(8,128)(2,1)S(1)} async-done(((bf16[128,64,128]{2,1,0:T(8,128)(2,1)}), bf16[128,64,128]{2,1,0:T(8,128)(2,1)S(1)}, u32[]{:S(2)}, u32[]{:S(2)}) %all-to-all-start.1) | async-done | bytes 2097184 | tf_op jit(solution)/shard_map/all_to_all | solution.py:230
  186.3 0.0 copy-start.3
  186.3 1.3 copy-done.3
  187.6 6.2 %shard_map.76 = bf16[2,64,64,128]{3,2,1,0:T(8,128)(2,1)} custom-call(f32[128]{0:T(128)} %gain_ref.1, bf16[128,64,128]{2,1,0:T(8,128)(2,1)} %copy-done.3, bf16[128,128]{1,0:T(8,128)(2,1)} %w_ref.3, bf16[2,64,64,128]{3,2,1,0:T(8,128)(2,1)} %shard_map.75.gate_hbm), custom_call_target="tpu_custom_call" | custom-call | tf_op jit(solution)/shard_map/pallas_call | solution.py:208
Async XLA Ops:
  150.4 5.6 %copy-start.1 = (bf16[128,128]{1,0:T(8,128)(2,1)S(1)}, bf16[128,128]{1,0:T(8,128)(2,1)}, u32[]{:S(2)}) copy-start(bf16[128,128]{1,0:T(8,128)(2,1)} %w_ref.2) | copy-start | bytes 98308
  150.5 5.6 %copy-start.2 = (s32[2048]{0:T(1024)S(1)}, s32[2048]{0:T(1024)}, u32[]{:S(2)}) copy-start(s32[2048]{0:T(1024)} %tok_ref.1) | copy-start | bytes 24580
  150.5 35.8 %all-to-all-start.1 = ((bf16[128,64,128]{2,1,0:T(8,128)(2,1)}), bf16[128,64,128]{2,1,0:T(8,128)(2,1)S(1)}, u32[]{:S(2)}, u32[]{:S(2)}) async-start(bf16[128,64,128]{2,1,0:T(8,128)(2,1)} %bitcast.8), calls=%async_computation.1 | async-start | bytes 4194304 | tf_op jit(solution)/shard_map/all_to_all | solution.py:230
  156.1 3.4 %copy-start = (bf16[128,256,128]{2,1,0:T(8,128)(2,1)S(1)}, bf16[128,256,128]{2,1,0:T(8,128)(2,1)}, u32[]{:S(2)}) copy-start(bf16[128,256,128]{2,1,0:T(8,128)(2,1)} %x_ref.1) | copy-start | bytes 25165828
  186.3 1.3 copy-start.3

commit v5 on v4

--- a/solution.py
+++ b/solution.py
@@ -8,6 +8,7 @@
 TOK_ROW = 128
 WIN_BLK = 32
 ROW_STEP = 16
+FINISH_STEP = 16
 PROJECT_VMEM = 48 << 20
 AXES = ("row", "chan")
 NT = (((1,), (1,)), ((), ()))
@@ -170,60 +171,58 @@
     return out.reshape(n_row * n_chan, half, 128)
 
 
-def finish_kernel(gain_ref, p_ref, w_ref, gate_hbm, o_ref, swap, gate_ref, sem):
+def finish_kernel(gain_ref, p_ref, w_ref, gate_hbm, o_hbm, swap, gate_ref, out, in_sem, out_sem):
     chans, subs, lanes = p_ref.shape
-    pitch = subs + 1
     half = lanes // 2
-    step = pl.program_id(0)
-
-    def gate_copy(n):
-        part = pl.ds(pl.multiple_of(n * subs, subs), subs)
-        return pltpu.make_async_copy(gate_hbm.at[:, part], gate_ref.at[n], sem.at[n])
-
-    @pl.when(step == 0)
-    def _():
-        for n in range(gate_ref.shape[0]):
-            gate_copy(n).start()
-
-    x = p_ref[...].astype(jnp.float32)
-    mean = jnp.sum(x, axis=0) * (1.0 / chans)
-    centred = x - mean[None]
-    var = jnp.sum(centred * centred, axis=0) * (1.0 / chans)
-    scale = lax.rsqrt(var + 1e-05)
-    for c in range(chans):
-        swap[c * pitch:c * pitch + subs, :] = centred[c] * scale * gain_ref[c]
-    gate_copy(step).wait()
-    for s in range(subs):
-        normed = swap[pl.ds(s, chans, stride=pitch), :].astype(jnp.bfloat16)
-        outcome = lax.dot_general(normed, w_ref[...], TN, preferred_element_type=jnp.float32)
-        for h in range(2):
-            gate = gate_ref[step, h, s].astype(jnp.float32)
-            o_ref[h, s] = (gate * outcome[h * half:(h + 1) * half]).astype(jnp.bfloat16)
+    parts = [pl.ds(first, FINISH_STEP) for first in range(0, subs, FINISH_STEP)]
+    pitch = FINISH_STEP + 1
+    gates = [
+        pltpu.make_async_copy(gate_hbm.at[:, part], gate_ref.at[:, part], in_sem.at[n]) for n, part in enumerate(parts)]
+    outs = [pltpu.make_async_copy(out.at[:, part], o_hbm.at[:, part], out_sem.at[n]) for n, part in enumerate(parts)]
+    for copy in gates:
+        copy.start()
+    for n, part in enumerate(parts):
+        x = p_ref[:, part].astype(jnp.float32)
+        mean = jnp.sum(x, axis=0) * (1.0 / chans)
+        centred = x - mean[None]
+        var = jnp.sum(centred * centred, axis=0) * (1.0 / chans)
+        scale = lax.rsqrt(var + 1e-05)
+        for c in range(chans):
+            swap[n % 2, c * pitch:c * pitch + FINISH_STEP, :] = centred[c] * scale * gain_ref[c]
+        gates[n].wait()
+        for s in range(FINISH_STEP):
+            normed = swap[n % 2, pl.ds(s, chans, stride=pitch), :].astype(jnp.bfloat16)
+            outcome = lax.dot_general(normed, w_ref[...], TN, preferred_element_type=jnp.float32)
+            for h in range(2):
+                gate = gate_ref[h, part.start + s].astype(jnp.float32)
+                out[h, part.start + s] = (gate * outcome[h * half:(h + 1) * half]).astype(jnp.bfloat16)
+        outs[n].start()
+    for copy in outs:
+        copy.wait()
 
 
 def finish(product, out_gain, w_out, gate):
     chans, subs, lanes = product.shape
-    rows, wins = 2 * subs, gate.shape[2]
-    step = 16
     out = pl.pallas_call(
         finish_kernel,
-        grid=(subs // step,),
         in_specs=[
             pl.BlockSpec(memory_space=pltpu.SMEM),
-            pl.BlockSpec((chans, step, lanes), lambda s: (0, s, 0)),
-            pl.BlockSpec((chans, chans), lambda s: (0, 0)),
+            pl.BlockSpec(memory_space=pltpu.VMEM),
+            pl.BlockSpec(memory_space=pltpu.VMEM),
             pl.BlockSpec(memory_space=pltpu.HBM),
         ],
-        out_specs=pl.BlockSpec((2, step, wins, chans), lambda s: (0, s, 0, 0)),
-        out_shape=pltpu.HBM((2, subs, wins, chans), jnp.bfloat16),
+        out_specs=pl.BlockSpec(memory_space=pltpu.HBM),
+        out_shape=pltpu.HBM(gate.shape, jnp.bfloat16),
         scratch_shapes=[
-            pltpu.VMEM((chans * (step + 1), lanes), jnp.float32),
-            pltpu.VMEM((subs // step, 2, step, wins, chans), jnp.bfloat16),
-            pltpu.SemaphoreType.DMA((subs // step,)),
-        ],
-        compiler_params=pltpu.CompilerParams(vmem_limit_bytes=60 << 20),
+            pltpu.VMEM((2, chans * (FINISH_STEP + 1), lanes), jnp.float32),
+            pltpu.VMEM(gate.shape, jnp.bfloat16),
+            pltpu.VMEM(gate.shape, jnp.bfloat16),
+            pltpu.SemaphoreType.DMA((subs // FINISH_STEP,)),
+            pltpu.SemaphoreType.DMA((subs // FINISH_STEP,)),
+        ],
+        compiler_params=pltpu.CompilerParams(vmem_limit_bytes=50 << 20),
     )(out_gain, product, w_out, gate)
-    return out.reshape(rows, wins, chans)
+    return out.reshape(2 * subs, gate.shape[2], chans)
 
 
 def spread(values):

time: 194 us -> 191 us (0.985)
    unnamed x8 -> x10, local copies, waits for them, and re-layouts: 4.73 us -> 3.4 us
where the time goes in v5:
time: 191 us
  blocking collectives  131 us (69%)
  Pallas kernels  28.4 us (15%)
  waiting for transfers between devices  22 us (12%)
  starting transfers between devices  5.6 us (3%)
  local copies, waits for them, and re-layouts  3.4 us (2%)
    all_to_all x1, blocking collectives, spread(): return lax.all_to_all(values, AXES, split_axis=0, concat_axis=0, tiled=True)  131 us
    all_to_all x1, waiting for transfers between devices, spread(): return lax.all_to_all(values, AXES, split_axis=0, concat_axis=0, tiled=True)  22 us
    pallas_call x1, Pallas kernels, project(): pl.pallas_call(project_kernel, grid=(rows // ROW_STEP,), in_specs=[pl.Blo...  13.7 us
    all_to_all x1, starting transfers between devices, spread(): return lax.all_to_all(values, AXES, split_axis=0, concat_axis=0, tiled=True)  5.6 us
    pallas_call x1, Pallas kernels, product_of(): pl.pallas_call(product_kernel, in_specs=[pl.BlockSpec(memory_space=pltpu....  5.43 us
    pallas_call x1, Pallas kernels, gate_of(): pl.pallas_call(gate_kernel, grid=(rows // 32,), in_specs=[pl.BlockSpec(me...  4.74 us
    pallas_call x1, Pallas kernels, finish(): pl.pallas_call(finish_kernel, in_specs=[pl.BlockSpec(memory_space=pltpu.S...  4.6 us
  transfers between devices with their start and end apart: 1, of which 1 were waited for; matrix products, arithmetic and copies ran while one was open for 0% of the time, Pallas kernels for 2%

profile of v5, /device:TPU:0, one launch (start us, length us, event | category | flops | bytes accessed | tf_op | source)
XLA Modules:
  0.0 190.9 jit_solution(3684204801006595920)
XLA Ops:
  0.0 13.7 %shard_map.73 = bf16[128,160,256]{2,1,0:T(8,128)(2,1)S(1)} custom-call(bf16[128,256,128]{2,1,0:T(8,128)(2,1)} %x_ref.1, bf16[128,256]{1,0:T(8,128)(2,1)} %left_ref.1, bf16[128,256]{1,0:T(8,128)(2,1)} %right_ref.1, s32[16,128]{1,0:T(8,128)} %bitcast.7), custom_call_target="tpu_custom_call" | custom-call | tf_op jit(solution)/shard_map/pallas_call | solution.py:67
  13.7 131.3 %all_to_all.10 = bf16[128,160,256]{2,1,0:T(8,128)(2,1)S(1)} all-to-all(bf16[128,160,256]{2,1,0:T(8,128)(2,1)S(1)} %shard_map.73), channel_id=1, replica_groups=mesh['row'=16,'chan'=8] {'row','chan'}, dimensions={0} | all-to-all | bytes 20971520 | tf_op jit(solution)/shard_map/all_to_all | solution.py:229
  145.0 5.4 %shard_map.74 = bf16[16,8,64,128]{3,2,1,0:T(8,128)(2,1)} custom-call(bf16[16,8,160,256]{3,2,1,0:T(8,128)(2,1)S(1)} %bitcast.5), custom_call_target="tpu_custom_call" | custom-call | tf_op jit(solution)/shard_map/pallas_call | solution.py:159
  150.4 0.0 copy-start.1
  150.5 0.0 copy-start.3
  150.5 5.6 %all-to-all-start.1 = ((bf16[128,64,128]{2,1,0:T(8,128)(2,1)}), bf16[128,64,128]{2,1,0:T(8,128)(2,1)S(1)}, u32[]{:S(2)}, u32[]{:S(2)}) async-start(bf16[128,64,128]{2,1,0:T(8,128)(2,1)} %bitcast.8), calls=%async_computation.1 | async-start | bytes 4194304 | tf_op jit(solution)/shard_map/all_to_all | solution.py:229
  156.1 0.0 copy-done.1
  156.1 0.0 copy-done.3
  156.1 0.0 copy-start
  156.1 3.4 %copy-done = bf16[128,256,128]{2,1,0:T(8,128)(2,1)S(1)} copy-done((bf16[128,256,128]{2,1,0:T(8,128)(2,1)S(1)}, bf16[128,256,128]{2,1,0:T(8,128)(2,1)}, u32[]{:S(2)}) %copy-start) | copy-done | bytes 8388632
  159.5 0.0 copy-start.2
  159.5 0.0 copy-start.4
  159.5 4.7 %shard_map.75.gate_hbm = bf16[2,64,64,128]{3,2,1,0:T(8,128)(2,1)} custom-call(s32[2048]{0:T(1024)S(1)} %copy-done.3, bf16[128,2,128,128]{3,2,1,0:T(8,128)(2,1)S(1)} %bitcast.6, bf16[128,128]{1,0:T(8,128)(2,1)S(1)} %copy-done.1), custom_call_target="tpu_custom_call" | custom-call | tf_op jit(solution)/shard_map/pallas_call | solution.py:108
  164.2 22.0 %all-to-all-done.1.p_ref = bf16[128,64,128]{2,1,0:T(8,128)(2,1)S(1)} async-done(((bf16[128,64,128]{2,1,0:T(8,128)(2,1)}), bf16[128,64,128]{2,1,0:T(8,128)(2,1)S(1)}, u32[]{:S(2)}, u32[]{:S(2)}) %all-to-all-start.1) | async-done | bytes 2097184 | tf_op jit(solution)/shard_map/all_to_all | solution.py:229
  186.3 0.0 copy-done.2
  186.3 0.0 copy-done.4
  186.3 4.6 %shard_map.76 = bf16[2,64,64,128]{3,2,1,0:T(8,128)(2,1)} custom-call(f32[128]{0:T(128)S(1)} %copy-done.4, bf16[128,64,128]{2,1,0:T(8,128)(2,1)S(1)} %all-to-all-done.1.p_ref, bf16[128,128]{1,0:T(8,128)(2,1)S(1)} %copy-done.2, bf16[2,64,64,128]{3,2,1,0:T(8,128)(2,1)} %shard_map.75.gate_hbm), custom_call_target="tpu_custom_call" | custom-call | tf_op jit(solution)/shard_map/pallas_call | solution.py:206
Async XLA Ops:
  150.4 5.6 %copy-start.1 = (bf16[128,128]{1,0:T(8,128)(2,1)S(1)}, bf16[128,128]{1,0:T(8,128)(2,1)}, u32[]{:S(2)}) copy-start(bf16[128,128]{1,0:T(8,128)(2,1)} %w_ref.2) | copy-start | bytes 98308
  150.5 5.6 %copy-start.3 = (s32[2048]{0:T(1024)S(1)}, s32[2048]{0:T(1024)}, u32[]{:S(2)}) copy-start(s32[2048]{0:T(1024)} %tok_ref.1) | copy-start | bytes 24580
  150.5 35.8 %all-to-all-start.1 = ((bf16[128,64,128]{2,1,0:T(8,128)(2,1)}), bf16[128,64,128]{2,1,0:T(8,128)(2,1)S(1)}, u32[]{:S(2)}, u32[]{:S(2)}) async-start(bf16[128,64,128]{2,1,0:T(8,128)(2,1)} %bitcast.8), calls=%async_computation.1 | async-start | bytes 4194304 | tf_op jit(solution)/shard_map/all_to_all | solution.py:229
  156.1 3.4 %copy-start = (bf16[128,256,128]{2,1,0:T(8,128)(2,1)S(1)}, bf16[128,256,128]{2,1,0:T(8,128)(2,1)}, u32[]{:S(2)}) copy-start(bf16[128,256,128]{2,1,0:T(8,128)(2,1)} %x_ref.1) | copy-start | bytes 25165828
  159.5 26.8 %copy-start.2 = (bf16[128,128]{1,0:T(8,128)(2,1)S(1)}, bf16[128,128]{1,0:T(8,128)(2,1)}, u32[]{:S(2)}) copy-start(bf16[128,128]{1,0:T(8,128)(2,1)} %w_ref.3) | copy-start | bytes 98308
  159.5 26.8 %copy-start.4 = (f32[128]{0:T(128)S(1)}, f32[128]{0:T(128)}, u32[]{:S(2)}) copy-start(f32[128]{0:T(128)} %gain_ref.1) | copy-start | bytes 1540

commit v6 on v5

--- a/solution.py
+++ b/solution.py
@@ -77,7 +77,7 @@
         out_shape=pltpu.VMEM((chans, WIN_BLK + rows, cols), jnp.bfloat16),
         scratch_shapes=[
             pltpu.VMEM((4 * chans, chans), jnp.bfloat16),
-            pltpu.VMEM((2, cols // 128, ROW_STEP * (chans + 1), 128), jnp.float32),
+            pltpu.VMEM((2, cols // 128, (ROW_STEP + 1) * (chans + 1), 128), jnp.float32),
         ],
         compiler_params=pltpu.CompilerParams(vmem_limit_bytes=PROJECT_VMEM),
     )(pair, w_left, w_right, tokens)
@@ -214,7 +214,7 @@
         out_specs=pl.BlockSpec(memory_space=pltpu.HBM),
         out_shape=pltpu.HBM(gate.shape, jnp.bfloat16),
         scratch_shapes=[
-            pltpu.VMEM((2, chans * (FINISH_STEP + 1), lanes), jnp.float32),
+            pltpu.VMEM((2, (chans + 1) * (FINISH_STEP + 1), lanes), jnp.float32),
             pltpu.VMEM(gate.shape, jnp.bfloat16),
             pltpu.VMEM(gate.shape, jnp.bfloat16),
             pltpu.SemaphoreType.DMA((subs // FINISH_STEP,)),

time: 191 us -> 191 us (level)
  no operation moved by 1% of the time
where the time goes in v6:
time: 191 us
  blocking collectives  131 us (69%)
  Pallas kernels  28.4 us (15%)
  waiting for transfers between devices  22 us (12%)
  starting transfers between devices  5.6 us (3%)
  local copies, waits for them, and re-layouts  3.4 us (2%)
    all_to_all x1, blocking collectives, spread(): return lax.all_to_all(values, AXES, split_axis=0, concat_axis=0, tiled=True)  131 us
    all_to_all x1, waiting for transfers between devices, spread(): return lax.all_to_all(values, AXES, split_axis=0, concat_axis=0, tiled=True)  22 us
    pallas_call x1, Pallas kernels, project(): pl.pallas_call(project_kernel, grid=(rows // ROW_STEP,), in_specs=[pl.Blo...  13.6 us
    all_to_all x1, starting transfers between devices, spread(): return lax.all_to_all(values, AXES, split_axis=0, concat_axis=0, tiled=True)  5.6 us
    pallas_call x1, Pallas kernels, product_of(): pl.pallas_call(product_kernel, in_specs=[pl.BlockSpec(memory_space=pltpu....  5.43 us
    pallas_call x1, Pallas kernels, gate_of(): pl.pallas_call(gate_kernel, grid=(rows // 32,), in_specs=[pl.BlockSpec(me...  4.74 us
    pallas_call x1, Pallas kernels, finish(): pl.pallas_call(finish_kernel, in_specs=[pl.BlockSpec(memory_space=pltpu.S...  4.61 us
  transfers between devices with their start and end apart: 1, of which 1 were waited for; matrix products, arithmetic and copies ran while one was open for 0% of the time, Pallas kernels for 2%

profile of v6, /device:TPU:0, one launch (start us, length us, event | category | flops | bytes accessed | tf_op | source)
XLA Modules:
  0.0 190.8 jit_solution(12607976294318695517)
XLA Ops:
  0.0 13.6 %shard_map.73 = bf16[128,160,256]{2,1,0:T(8,128)(2,1)S(1)} custom-call(bf16[128,256,128]{2,1,0:T(8,128)(2,1)} %x_ref.1, bf16[128,256]{1,0:T(8,128)(2,1)} %left_ref.1, bf16[128,256]{1,0:T(8,128)(2,1)} %right_ref.1, s32[16,128]{1,0:T(8,128)} %bitcast.7), custom_call_target="tpu_custom_call" | custom-call | tf_op jit(solution)/shard_map/pallas_call | solution.py:67
  13.6 131.3 %all_to_all.10 = bf16[128,160,256]{2,1,0:T(8,128)(2,1)S(1)} all-to-all(bf16[128,160,256]{2,1,0:T(8,128)(2,1)S(1)} %shard_map.73), channel_id=1, replica_groups=mesh['row'=16,'chan'=8] {'row','chan'}, dimensions={0} | all-to-all | bytes 20971520 | tf_op jit(solution)/shard_map/all_to_all | solution.py:229
  145.0 5.4 %shard_map.74 = bf16[16,8,64,128]{3,2,1,0:T(8,128)(2,1)} custom-call(bf16[16,8,160,256]{3,2,1,0:T(8,128)(2,1)S(1)} %bitcast.5), custom_call_target="tpu_custom_call" | custom-call | tf_op jit(solution)/shard_map/pallas_call | solution.py:159
  150.4 0.0 copy-start.1
  150.4 0.0 copy-start.3
  150.4 5.6 %all-to-all-start.1 = ((bf16[128,64,128]{2,1,0:T(8,128)(2,1)}), bf16[128,64,128]{2,1,0:T(8,128)(2,1)S(1)}, u32[]{:S(2)}, u32[]{:S(2)}) async-start(bf16[128,64,128]{2,1,0:T(8,128)(2,1)} %bitcast.8), calls=%async_computation.1 | async-start | bytes 4194304 | tf_op jit(solution)/shard_map/all_to_all | solution.py:229
  156.0 0.0 copy-done.1
  156.0 0.0 copy-done.3
  156.0 0.0 copy-start
  156.1 3.4 %copy-done = bf16[128,256,128]{2,1,0:T(8,128)(2,1)S(1)} copy-done((bf16[128,256,128]{2,1,0:T(8,128)(2,1)S(1)}, bf16[128,256,128]{2,1,0:T(8,128)(2,1)}, u32[]{:S(2)}) %copy-start) | copy-done | bytes 8388632
  159.4 0.0 copy-start.2
  159.4 0.0 copy-start.4
  159.4 4.7 %shard_map.75.gate_hbm = bf16[2,64,64,128]{3,2,1,0:T(8,128)(2,1)} custom-call(s32[2048]{0:T(1024)S(1)} %copy-done.3, bf16[128,2,128,128]{3,2,1,0:T(8,128)(2,1)S(1)} %bitcast.6, bf16[128,128]{1,0:T(8,128)(2,1)S(1)} %copy-done.1), custom_call_target="tpu_custom_call" | custom-call | tf_op jit(solution)/shard_map/pallas_call | solution.py:108
  164.2 22.0 %all-to-all-done.1.p_ref = bf16[128,64,128]{2,1,0:T(8,128)(2,1)S(1)} async-done(((bf16[128,64,128]{2,1,0:T(8,128)(2,1)}), bf16[128,64,128]{2,1,0:T(8,128)(2,1)S(1)}, u32[]{:S(2)}, u32[]{:S(2)}) %all-to-all-start.1) | async-done | bytes 2097184 | tf_op jit(solution)/shard_map/all_to_all | solution.py:229
  186.2 0.0 copy-done.2
  186.2 0.0 copy-done.4
  186.2 4.6 %shard_map.76 = bf16[2,64,64,128]{3,2,1,0:T(8,128)(2,1)} custom-call(f32[128]{0:T(128)S(1)} %copy-done.4, bf16[128,64,128]{2,1,0:T(8,128)(2,1)S(1)} %all-to-all-done.1.p_ref, bf16[128,128]{1,0:T(8,128)(2,1)S(1)} %copy-done.2, bf16[2,64,64,128]{3,2,1,0:T(8,128)(2,1)} %shard_map.75.gate_hbm), custom_call_target="tpu_custom_call" | custom-call | tf_op jit(solution)/shard_map/pallas_call | solution.py:206
Async XLA Ops:
  150.4 5.6 %copy-start.1 = (bf16[128,128]{1,0:T(8,128)(2,1)S(1)}, bf16[128,128]{1,0:T(8,128)(2,1)}, u32[]{:S(2)}) copy-start(bf16[128,128]{1,0:T(8,128)(2,1)} %w_ref.2) | copy-start | bytes 98308
  150.4 5.6 %copy-start.3 = (s32[2048]{0:T(1024)S(1)}, s32[2048]{0:T(1024)}, u32[]{:S(2)}) copy-start(s32[2048]{0:T(1024)} %tok_ref.1) | copy-start | bytes 24580
  150.4 35.8 %all-to-all-start.1 = ((bf16[128,64,128]{2,1,0:T(8,128)(2,1)}), bf16[128,64,128]{2,1,0:T(8,128)(2,1)S(1)}, u32[]{:S(2)}, u32[]{:S(2)}) async-start(bf16[128,64,128]{2,1,0:T(8,128)(2,1)} %bitcast.8), calls=%async_computation.1 | async-start | bytes 4194304 | tf_op jit(solution)/shard_map/all_to_all | solution.py:229
  156.0 3.4 %copy-start = (bf16[128,256,128]{2,1,0:T(8,128)(2,1)S(1)}, bf16[128,256,128]{2,1,0:T(8,128)(2,1)}, u32[]{:S(2)}) copy-start(bf16[128,256,128]{2,1,0:T(8,128)(2,1)} %x_ref.1) | copy-start | bytes 25165828
  159.4 26.8 %copy-start.2 = (bf16[128,128]{1,0:T(8,128)(2,1)S(1)}, bf16[128,128]{1,0:T(8,128)(2,1)}, u32[]{:S(2)}) copy-start(bf16[128,128]{1,0:T(8,128)(2,1)} %w_ref.3) | copy-start | bytes 98308
  159.4 26.8 %copy-start.4 = (f32[128]{0:T(128)S(1)}, f32[128]{0:T(128)}, u32[]{:S(2)}) copy-start(f32[128]{0:T(128)} %gain_ref.1) | copy-start | bytes 1540

commit v7 on v6

--- a/solution.py
+++ b/solution.py
@@ -9,6 +9,7 @@
 WIN_BLK = 32
 ROW_STEP = 16
 FINISH_STEP = 16
+SEND_STEP = 4
 PROJECT_VMEM = 48 << 20
 AXES = ("row", "chan")
 NT = (((1,), (1,)), ((), ()))
@@ -143,9 +144,8 @@
                 bot = acc[r * rows + half:(r + 1) * rows, m * 128:(m + 1) * 128]
                 out[first + r, 2 * m] = jnp.where(low, top, pltpu.roll(bot, 64, 1)).astype(jnp.bfloat16)
                 out[first + r, 2 * m + 1] = jnp.where(low, pltpu.roll(top, 64, 1), bot).astype(jnp.bfloat16)
-        part = pl.ds(first, steps)
-        copies.append(pltpu.make_async_copy(out.at[part], o_hbm.at[part], sem.at[first // steps]))
-        copies[-1].start()
+            copies.append(pltpu.make_async_copy(out.at[first + r], o_hbm.at[first + r], sem.at[first + r]))
+            copies[-1].start()
     for copy in copies:
         copy.wait()
 
@@ -164,7 +164,7 @@
         scratch_shapes=[
             pltpu.VMEM((steps * 2 * half, n_row * WIN_BLK), jnp.float32),
             pltpu.VMEM(shape, jnp.bfloat16),
-            pltpu.SemaphoreType.DMA((n_row // steps,)),
+            pltpu.SemaphoreType.DMA((n_row,)),
         ],
         compiler_params=pltpu.CompilerParams(vmem_limit_bytes=16 << 20),
     )(sides.reshape(n_row, n_chan, rows, depth))
@@ -178,7 +178,8 @@
     pitch = FINISH_STEP + 1
     gates = [
         pltpu.make_async_copy(gate_hbm.at[:, part], gate_ref.at[:, part], in_sem.at[n]) for n, part in enumerate(parts)]
-    outs = [pltpu.make_async_copy(out.at[:, part], o_hbm.at[:, part], out_sem.at[n]) for n, part in enumerate(parts)]
+    sends = [pl.ds(first, SEND_STEP) for first in range(0, subs, SEND_STEP)]
+    outs = [pltpu.make_async_copy(out.at[:, part], o_hbm.at[:, part], out_sem.at[n]) for n, part in enumerate(sends)]
     for copy in gates:
         copy.start()
     for n, part in enumerate(parts):
@@ -196,7 +197,8 @@
             for h in range(2):
                 gate = gate_ref[h, part.start + s].astype(jnp.float32)
                 out[h, part.start + s] = (gate * outcome[h * half:(h + 1) * half]).astype(jnp.bfloat16)
-        outs[n].start()
+            if (s + 1) % SEND_STEP == 0:
+                outs[(part.start + s) // SEND_STEP].start()
     for copy in outs:
         copy.wait()
 
@@ -218,7 +220,7 @@
             pltpu.VMEM(gate.shape, jnp.bfloat16),
             pltpu.VMEM(gate.shape, jnp.bfloat16),
             pltpu.SemaphoreType.DMA((subs // FINISH_STEP,)),
-            pltpu.SemaphoreType.DMA((subs // FINISH_STEP,)),
+            pltpu.SemaphoreType.DMA((subs // SEND_STEP,)),
         ],
         compiler_params=pltpu.CompilerParams(vmem_limit_bytes=50 << 20),
     )(out_gain, product, w_out, gate)

time: 191 us -> 191 us (level)
  no operation moved by 1% of the time
where the time goes in v7:
time: 191 us
  blocking collectives  131 us (69%)
  Pallas kernels  28.4 us (15%)
  waiting for transfers between devices  22 us (12%)
  starting transfers between devices  5.6 us (3%)
  local copies, waits for them, and re-layouts  3.4 us (2%)
    all_to_all x1, blocking collectives, spread(): return lax.all_to_all(values, AXES, split_axis=0, concat_axis=0, tiled=True)  131 us
    all_to_all x1, waiting for transfers between devices, spread(): return lax.all_to_all(values, AXES, split_axis=0, concat_axis=0, tiled=True)  22 us
    pallas_call x1, Pallas kernels, project(): pl.pallas_call(project_kernel, grid=(rows // ROW_STEP,), in_specs=[pl.Blo...  13.6 us
    all_to_all x1, starting transfers between devices, spread(): return lax.all_to_all(values, AXES, split_axis=0, concat_axis=0, tiled=True)  5.6 us
    pallas_call x1, Pallas kernels, product_of(): pl.pallas_call(product_kernel, in_specs=[pl.BlockSpec(memory_space=pltpu....  5.42 us
    pallas_call x1, Pallas kernels, gate_of(): pl.pallas_call(gate_kernel, grid=(rows // 32,), in_specs=[pl.BlockSpec(me...  4.74 us
    pallas_call x1, Pallas kernels, finish(): pl.pallas_call(finish_kernel, in_specs=[pl.BlockSpec(memory_space=pltpu.S...  4.55 us
  transfers between devices with their start and end apart: 1, of which 1 were waited for; matrix products, arithmetic and copies ran while one was open for 0% of the time, Pallas kernels for 2%

profile of v7, /device:TPU:0, one launch (start us, length us, event | category | flops | bytes accessed | tf_op | source)
XLA Modules:
  0.0 190.8 jit_solution(13228567716753124866)
XLA Ops:
  0.0 13.6 %shard_map.73 = bf16[128,160,256]{2,1,0:T(8,128)(2,1)S(1)} custom-call(bf16[128,256,128]{2,1,0:T(8,128)(2,1)} %x_ref.1, bf16[128,256]{1,0:T(8,128)(2,1)} %left_ref.1, bf16[128,256]{1,0:T(8,128)(2,1)} %right_ref.1, s32[16,128]{1,0:T(8,128)} %bitcast.7), custom_call_target="tpu_custom_call" | custom-call | tf_op jit(solution)/shard_map/pallas_call | solution.py:68
  13.6 131.3 %all_to_all.10 = bf16[128,160,256]{2,1,0:T(8,128)(2,1)S(1)} all-to-all(bf16[128,160,256]{2,1,0:T(8,128)(2,1)S(1)} %shard_map.73), channel_id=1, replica_groups=mesh['row'=16,'chan'=8] {'row','chan'}, dimensions={0} | all-to-all | bytes 20971520 | tf_op jit(solution)/shard_map/all_to_all | solution.py:231
  145.0 5.4 %shard_map.74 = bf16[16,8,64,128]{3,2,1,0:T(8,128)(2,1)} custom-call(bf16[16,8,160,256]{3,2,1,0:T(8,128)(2,1)S(1)} %bitcast.5), custom_call_target="tpu_custom_call" | custom-call | tf_op jit(solution)/shard_map/pallas_call | solution.py:159
  150.4 0.0 copy-start.1
  150.4 0.0 copy-start.3
  150.4 5.6 %all-to-all-start.1 = ((bf16[128,64,128]{2,1,0:T(8,128)(2,1)}), bf16[128,64,128]{2,1,0:T(8,128)(2,1)S(1)}, u32[]{:S(2)}, u32[]{:S(2)}) async-start(bf16[128,64,128]{2,1,0:T(8,128)(2,1)} %bitcast.8), calls=%async_computation.1 | async-start | bytes 4194304 | tf_op jit(solution)/shard_map/all_to_all | solution.py:231
  156.0 0.0 copy-done.1
  156.0 0.0 copy-done.3
  156.0 0.0 copy-start
  156.0 3.4 %copy-done = bf16[128,256,128]{2,1,0:T(8,128)(2,1)S(1)} copy-done((bf16[128,256,128]{2,1,0:T(8,128)(2,1)S(1)}, bf16[128,256,128]{2,1,0:T(8,128)(2,1)}, u32[]{:S(2)}) %copy-start) | copy-done | bytes 8388632
  159.4 0.0 copy-start.2
  159.4 0.0 copy-start.4
  159.4 4.7 %shard_map.75.gate_hbm = bf16[2,64,64,128]{3,2,1,0:T(8,128)(2,1)} custom-call(s32[2048]{0:T(1024)S(1)} %copy-done.3, bf16[128,2,128,128]{3,2,1,0:T(8,128)(2,1)S(1)} %bitcast.6, bf16[128,128]{1,0:T(8,128)(2,1)S(1)} %copy-done.1), custom_call_target="tpu_custom_call" | custom-call | tf_op jit(solution)/shard_map/pallas_call | solution.py:109
  164.2 22.0 %all-to-all-done.1.p_ref = bf16[128,64,128]{2,1,0:T(8,128)(2,1)S(1)} async-done(((bf16[128,64,128]{2,1,0:T(8,128)(2,1)}), bf16[128,64,128]{2,1,0:T(8,128)(2,1)S(1)}, u32[]{:S(2)}, u32[]{:S(2)}) %all-to-all-start.1) | async-done | bytes 2097184 | tf_op jit(solution)/shard_map/all_to_all | solution.py:231
  186.2 0.0 copy-done.2
  186.2 0.0 copy-done.4
  186.2 4.6 %shard_map.76 = bf16[2,64,64,128]{3,2,1,0:T(8,128)(2,1)} custom-call(f32[128]{0:T(128)S(1)} %copy-done.4, bf16[128,64,128]{2,1,0:T(8,128)(2,1)S(1)} %all-to-all-done.1.p_ref, bf16[128,128]{1,0:T(8,128)(2,1)S(1)} %copy-done.2, bf16[2,64,64,128]{3,2,1,0:T(8,128)(2,1)} %shard_map.75.gate_hbm), custom_call_target="tpu_custom_call" | custom-call | tf_op jit(solution)/shard_map/pallas_call | solution.py:208
Async XLA Ops:
  150.4 5.6 %copy-start.1 = (bf16[128,128]{1,0:T(8,128)(2,1)S(1)}, bf16[128,128]{1,0:T(8,128)(2,1)}, u32[]{:S(2)}) copy-start(bf16[128,128]{1,0:T(8,128)(2,1)} %w_ref.2) | copy-start | bytes 98308
  150.4 5.6 %copy-start.3 = (s32[2048]{0:T(1024)S(1)}, s32[2048]{0:T(1024)}, u32[]{:S(2)}) copy-start(s32[2048]{0:T(1024)} %tok_ref.1) | copy-start | bytes 24580
  150.4 35.8 %all-to-all-start.1 = ((bf16[128,64,128]{2,1,0:T(8,128)(2,1)}), bf16[128,64,128]{2,1,0:T(8,128)(2,1)S(1)}, u32[]{:S(2)}, u32[]{:S(2)}) async-start(bf16[128,64,128]{2,1,0:T(8,128)(2,1)} %bitcast.8), calls=%async_computation.1 | async-start | bytes 4194304 | tf_op jit(solution)/shard_map/all_to_all | solution.py:231
  156.0 3.4 %copy-start = (bf16[128,256,128]{2,1,0:T(8,128)(2,1)S(1)}, bf16[128,256,128]{2,1,0:T(8,128)(2,1)}, u32[]{:S(2)}) copy-start(bf16[128,256,128]{2,1,0:T(8,128)(2,1)} %x_ref.1) | copy-start | bytes 25165828
  159.4 26.8 %copy-start.2 = (bf16[128,128]{1,0:T(8,128)(2,1)S(1)}, bf16[128,128]{1,0:T(8,128)(2,1)}, u32[]{:S(2)}) copy-start(bf16[128,128]{1,0:T(8,128)(2,1)} %w_ref.3) | copy-start | bytes 98308
  159.4 26.8 %copy-start.4 = (f32[128]{0:T(128)S(1)}, f32[128]{0:T(128)}, u32[]{:S(2)}) copy-start(f32[128]{0:T(128)} %gain_ref.1) | copy-start | bytes 1540

commit v8 on v6

--- a/solution.py
+++ b/solution.py
@@ -129,14 +129,10 @@
     low = lax.broadcasted_iota(jnp.int32, (half, 128), 1) < 64
     copies = []
     for first in range(0, n_row, steps):
-        for q in range(n_chan):
-            term = lax.dot_general(
-                x_ref[first:first + steps, q, WIN_BLK:].reshape(steps * rows, depth),
-                x_ref[:, q, :WIN_BLK].reshape(wins, depth), NT, preferred_element_type=jnp.float32)
-            if q == 0:
-                acc[...] = term
-            else:
-                acc[...] += term
+        left = [x_ref[first:first + steps, q, WIN_BLK:].reshape(steps * rows, depth) for q in range(n_chan)]
+        right = [x_ref[:, q, :WIN_BLK].reshape(wins, depth) for q in range(n_chan)]
+        acc[...] = lax.dot_general(
+            jnp.concatenate(left, axis=1), jnp.concatenate(right, axis=1), NT, preferred_element_type=jnp.float32)
         for r in range(steps):
             for m in range(wins // 128):
                 top = acc[r * rows:r * rows + half, m * 128:(m + 1) * 128]

time: 191 us -> 191 us (level)
  no operation moved by 1% of the time
where the time goes in v8:
time: 191 us
  blocking collectives  131 us (69%)
  Pallas kernels  28.4 us (15%)
  waiting for transfers between devices  22 us (12%)
  starting transfers between devices  5.6 us (3%)
  local copies, waits for them, and re-layouts  3.4 us (2%)
    all_to_all x1, blocking collectives, spread(): return lax.all_to_all(values, AXES, split_axis=0, concat_axis=0, tiled=True)  131 us
    all_to_all x1, waiting for transfers between devices, spread(): return lax.all_to_all(values, AXES, split_axis=0, concat_axis=0, tiled=True)  22 us
    pallas_call x1, Pallas kernels, project(): pl.pallas_call(project_kernel, grid=(rows // ROW_STEP,), in_specs=[pl.Blo...  13.6 us
    all_to_all x1, starting transfers between devices, spread(): return lax.all_to_all(values, AXES, split_axis=0, concat_axis=0, tiled=True)  5.6 us
    pallas_call x1, Pallas kernels, product_of(): pl.pallas_call(product_kernel, in_specs=[pl.BlockSpec(memory_space=pltpu....  5.43 us
    pallas_call x1, Pallas kernels, gate_of(): pl.pallas_call(gate_kernel, grid=(rows // 32,), in_specs=[pl.BlockSpec(me...  4.74 us
    pallas_call x1, Pallas kernels, finish(): pl.pallas_call(finish_kernel, in_specs=[pl.BlockSpec(memory_space=pltpu.S...  4.61 us
  transfers between devices with their start and end apart: 1, of which 1 were waited for; matrix products, arithmetic and copies ran while one was open for 0% of the time, Pallas kernels for 2%

profile of v8, /device:TPU:0, one launch (start us, length us, event | category | flops | bytes accessed | tf_op | source)
XLA Modules:
  0.0 190.8 jit_solution(12607976294318695517)
XLA Ops:
  0.0 13.6 %shard_map.73 = bf16[128,160,256]{2,1,0:T(8,128)(2,1)S(1)} custom-call(bf16[128,256,128]{2,1,0:T(8,128)(2,1)} %x_ref.1, bf16[128,256]{1,0:T(8,128)(2,1)} %left_ref.1, bf16[128,256]{1,0:T(8,128)(2,1)} %right_ref.1, s32[16,128]{1,0:T(8,128)} %bitcast.7), custom_call_target="tpu_custom_call" | custom-call | tf_op jit(solution)/shard_map/pallas_call | solution.py:67
  13.6 131.3 %all_to_all.10 = bf16[128,160,256]{2,1,0:T(8,128)(2,1)S(1)} all-to-all(bf16[128,160,256]{2,1,0:T(8,128)(2,1)S(1)} %shard_map.73), channel_id=1, replica_groups=mesh['row'=16,'chan'=8] {'row','chan'}, dimensions={0} | all-to-all | bytes 20971520 | tf_op jit(solution)/shard_map/all_to_all | solution.py:225
  145.0 5.4 %shard_map.74 = bf16[16,8,64,128]{3,2,1,0:T(8,128)(2,1)} custom-call(bf16[16,8,160,256]{3,2,1,0:T(8,128)(2,1)S(1)} %bitcast.5), custom_call_target="tpu_custom_call" | custom-call | tf_op jit(solution)/shard_map/pallas_call | solution.py:155
  150.4 0.0 copy-start.1
  150.4 0.0 copy-start.3
  150.4 5.6 %all-to-all-start.1 = ((bf16[128,64,128]{2,1,0:T(8,128)(2,1)}), bf16[128,64,128]{2,1,0:T(8,128)(2,1)S(1)}, u32[]{:S(2)}, u32[]{:S(2)}) async-start(bf16[128,64,128]{2,1,0:T(8,128)(2,1)} %bitcast.8), calls=%async_computation.1 | async-start | bytes 4194304 | tf_op jit(solution)/shard_map/all_to_all | solution.py:225
  156.0 0.0 copy-done.1
  156.0 0.0 copy-done.3
  156.0 0.0 copy-start
  156.1 3.4 %copy-done = bf16[128,256,128]{2,1,0:T(8,128)(2,1)S(1)} copy-done((bf16[128,256,128]{2,1,0:T(8,128)(2,1)S(1)}, bf16[128,256,128]{2,1,0:T(8,128)(2,1)}, u32[]{:S(2)}) %copy-start) | copy-done | bytes 8388632
  159.4 0.0 copy-start.2
  159.4 0.0 copy-start.4
  159.4 4.7 %shard_map.75.gate_hbm = bf16[2,64,64,128]{3,2,1,0:T(8,128)(2,1)} custom-call(s32[2048]{0:T(1024)S(1)} %copy-done.3, bf16[128,2,128,128]{3,2,1,0:T(8,128)(2,1)S(1)} %bitcast.6, bf16[128,128]{1,0:T(8,128)(2,1)S(1)} %copy-done.1), custom_call_target="tpu_custom_call" | custom-call | tf_op jit(solution)/shard_map/pallas_call | solution.py:108
  164.2 22.0 %all-to-all-done.1.p_ref = bf16[128,64,128]{2,1,0:T(8,128)(2,1)S(1)} async-done(((bf16[128,64,128]{2,1,0:T(8,128)(2,1)}), bf16[128,64,128]{2,1,0:T(8,128)(2,1)S(1)}, u32[]{:S(2)}, u32[]{:S(2)}) %all-to-all-start.1) | async-done | bytes 2097184 | tf_op jit(solution)/shard_map/all_to_all | solution.py:225
  186.2 0.0 copy-done.2
  186.2 0.0 copy-done.4
  186.2 4.6 %shard_map.76 = bf16[2,64,64,128]{3,2,1,0:T(8,128)(2,1)} custom-call(f32[128]{0:T(128)S(1)} %copy-done.4, bf16[128,64,128]{2,1,0:T(8,128)(2,1)S(1)} %all-to-all-done.1.p_ref, bf16[128,128]{1,0:T(8,128)(2,1)S(1)} %copy-done.2, bf16[2,64,64,128]{3,2,1,0:T(8,128)(2,1)} %shard_map.75.gate_hbm), custom_call_target="tpu_custom_call" | custom-call | tf_op jit(solution)/shard_map/pallas_call | solution.py:202
Async XLA Ops:
  150.4 5.6 %copy-start.1 = (bf16[128,128]{1,0:T(8,128)(2,1)S(1)}, bf16[128,128]{1,0:T(8,128)(2,1)}, u32[]{:S(2)}) copy-start(bf16[128,128]{1,0:T(8,128)(2,1)} %w_ref.2) | copy-start | bytes 98308
  150.4 5.6 %copy-start.3 = (s32[2048]{0:T(1024)S(1)}, s32[2048]{0:T(1024)}, u32[]{:S(2)}) copy-start(s32[2048]{0:T(1024)} %tok_ref.1) | copy-start | bytes 24580
  150.4 35.8 %all-to-all-start.1 = ((bf16[128,64,128]{2,1,0:T(8,128)(2,1)}), bf16[128,64,128]{2,1,0:T(8,128)(2,1)S(1)}, u32[]{:S(2)}, u32[]{:S(2)}) async-start(bf16[128,64,128]{2,1,0:T(8,128)(2,1)} %bitcast.8), calls=%async_computation.1 | async-start | bytes 4194304 | tf_op jit(solution)/shard_map/all_to_all | solution.py:225
  156.0 3.4 %copy-start = (bf16[128,256,128]{2,1,0:T(8,128)(2,1)S(1)}, bf16[128,256,128]{2,1,0:T(8,128)(2,1)}, u32[]{:S(2)}) copy-start(bf16[128,256,128]{2,1,0:T(8,128)(2,1)} %x_ref.1) | copy-start | bytes 25165828
  159.4 26.8 %copy-start.2 = (bf16[128,128]{1,0:T(8,128)(2,1)S(1)}, bf16[128,128]{1,0:T(8,128)(2,1)}, u32[]{:S(2)}) copy-start(bf16[128,128]{1,0:T(8,128)(2,1)} %w_ref.3) | copy-start | bytes 98308
  159.4 26.8 %copy-start.4 = (f32[128]{0:T(128)S(1)}, f32[128]{0:T(128)}, u32[]{:S(2)}) copy-start(f32[128]{0:T(128)} %gain_ref.1) | copy-start | bytes 1540
